TPU v7x, 256 devices: a whole 4x4x8 slice. The times are simulated.
256 devices in a mesh: samp: 64 (over x_hi, y, z), par: 4 (over x_lo, core).
Axes of the slice: x: 4 (x_hi: 2, x_lo: 2; x = x_hi * 2 + x_lo), y: 4, z: 8, core: 2. Of those that a mesh axis runs over, the one named last changes fastest.
Arguments:
- spin_bits: int32 [1024, 100], P('samp'), may hold values from 0 to 1
- flip_energy: float32 [1024], P('samp'), may hold values from -8 to 8
- jacobian: bfloat16 [1024, 786432], P('samp', 'par')
Outputs:
- update: float32 [4, 64, 3072], P('par', 'samp')
All inputs are finite; a program needn't handle non-finite values.
Results may differ from a plain program's by a relative error of at most 0.002.
The roundings to bfloat16 on the way count: a program that leaves them out, or rounds other values in their place, can miss the bound.
Values may be sent and summed in bfloat16 or wider, within the bound.
A program may use at most 128 MiB of HBM per device.

v0:
```python
import math

import jax
import jax.numpy as jnp
from jax import lax
from jax.sharding import PartitionSpec as P

SITES = 100


diag_shift = 0.5
coupling_one = 1.0
coupling_two = 0.5


def diagonal_energy(spin_bits):
    lattice_side = math.isqrt(SITES)
    spin_signs = (2 * spin_bits - 1).astype(jnp.float32).reshape(-1, lattice_side, lattice_side)
    east_spins = jnp.roll(spin_signs, -1, axis=2)
    south_spins = jnp.roll(spin_signs, -1, axis=1)
    nearest = jnp.sum(spin_signs * east_spins + spin_signs * south_spins, axis=(1, 2))
    diagonal_one = jnp.roll(south_spins, -1, axis=2)
    diagonal_two = jnp.roll(south_spins, 1, axis=2)
    further = jnp.sum(spin_signs * diagonal_one + spin_signs * diagonal_two, axis=(1, 2))
    return 0.25 * coupling_one * nearest + 0.25 * coupling_two * further


def solve_both(factor, right_side):
    middle = lax.linalg.triangular_solve(factor, right_side[:, None], left_side=True, lower=True)
    result = lax.linalg.triangular_solve(
        factor, middle, left_side=True, lower=True, transpose_a=True
    )
    return result[:, 0]


def on_device(spin_bits, flip_energy, jacobian):
    energy = diagonal_energy(spin_bits) + flip_energy
    every_energy = lax.all_gather(energy, "samp", axis=0, tiled=True)
    centred_energy = every_energy - jnp.mean(every_energy)
    columns = lax.all_to_all(jacobian, "samp", split_axis=1, concat_axis=0, tiled=True)
    sample_count = columns.shape[0]
    column_mean = jnp.sum(columns, axis=0, dtype=jnp.float32) / sample_count
    centred = (columns.astype(jnp.float32) - column_mean[None, :]).astype(jnp.bfloat16)
    part_gram = lax.dot_general(
        centred, centred, (((1,), (1,)), ((), ())), preferred_element_type=jnp.float32
    )
    gram_total = lax.psum(part_gram, ("samp", "par"))
    shifted = gram_total + diag_shift * jnp.eye(sample_count, dtype=jnp.float32)
    factor = jnp.linalg.cholesky(shifted)
    weights = solve_both(factor, centred_energy).astype(jnp.bfloat16)
    direction = jnp.dot(weights, centred, preferred_element_type=jnp.float32)
    square_sum = lax.psum(jnp.sum(direction * direction), ("samp", "par"))
    params_total = lax.axis_size("par") * jacobian.shape[1]
    root_mean = jnp.sqrt(square_sum / params_total + 1e-06)
    return (-direction / root_mean).reshape(1, 1, -1)


def solution(mesh):
    return jax.shard_map(
        on_device,
        mesh=mesh,
        in_specs=(P("samp", None), P("samp"), P("samp", "par")),
        out_specs=P("par", "samp", None),
        check_vma=False,
    )
```

profile of v0, /device:TPU:1, one launch (start us, length us, event | category | flops | bytes accessed | tf_op | source)
XLA Modules:
  0.0 884.1 jit_solution(8252701779530970012)
XLA Ops:
  6.5 3.2 copy.26
  9.8 153.4 %all_to_all.13 = bf16[16,64,3072]{2,0,1:T(8,128)(2,1)S(1)} all-to-all(bf16[16,64,3072]{2,0,1:T(8,128)(2,1)S(1)} %bitcast.368), channel_id=1, replica_groups=mesh['samp'=64,'par'=4] {'samp'}, dimensions={1} | all-to-all | bytes 12582912 | tf_op jit(solution)/shard_map/all_to_all | solution.py:40
  166.1 2.7 copy-done
  168.7 8.2 fusion.132
  179.7 154.1 %all-reduce.1 = f32[1024]{0:T(1024)S(1)} all-reduce(f32[1024]{0:T(1024)S(1)} %add_dynamic-update-slice_fusion), channel_id=1, replica_groups=mesh['samp'=64,'par'=4] {'samp'}, use_global_device_ids=true, to_apply=%add.1 | all-reduce | flops 1024 | bytes 8192
  335.1 108.6 %all-reduce.4.cloned.1.call-done = f32[1024,1024]{1,0:T(8,128)} async-done(((f32[1024,1024]{1,0:T(8,128)}), f32[1024,1024]{1,0:T(8,128)}) %all-reduce.4.cloned.1.call-update) | async-done | bytes 4194320 | tf_op jit(solution)/shard_map/psum | solution.py:47
  443.7 4.8 select_add_fusion
  448.6 5.5 copy.20
  454.1 4.5 fusion.1
  460.6 11.7 %cholesky.222 = f32[128,128]{1,0:T(8,128)S(1)} custom-call(f32[128,128]{1,0:T(8,128)S(1)} %cholesky.577), custom_call_target="Cholesky" | custom-call | tf_op jit(solution)/shard_map/jit(cholesky)/cholesky | solution.py:49
  472.3 2.6 cholesky.254
  474.9 9.8 %custom-call.64 = f32[1,128,128]{1,2,0:T(8,128)S(1)} custom-call(f32[1,128,128]{2,1,0:T(8,128)S(1)} %get-tuple-element.50), custom_call_target="InvertDiagBlocksLowerTriangular" | custom-call | tf_op jit(solution)/shard_map/jit(cholesky)/cholesky | solution.py:49
  488.6 11.9 %cholesky.243 = f32[128,128]{1,0:T(8,128)S(1)} custom-call(f32[128,128]{1,0:T(8,128)S(1)} %cholesky.581), custom_call_target="Cholesky" | custom-call | tf_op jit(solution)/shard_map/jit(cholesky)/cholesky | solution.py:49
  501.2 9.8 %custom-call.65 = f32[1,128,128]{1,2,0:T(8,128)S(1)} custom-call(f32[1,128,128]{2,1,0:T(8,128)S(1)} %get-tuple-element.47), custom_call_target="InvertDiagBlocksLowerTriangular" | custom-call | tf_op jit(solution)/shard_map/jit(cholesky)/cholesky | solution.py:49
  514.3 11.7 %cholesky.466 = f32[128,128]{1,0:T(8,128)S(1)} custom-call(f32[128,128]{1,0:T(8,128)S(1)} %cholesky.586), custom_call_target="Cholesky" | custom-call | tf_op jit(solution)/shard_map/jit(cholesky)/cholesky | solution.py:49
  527.4 9.8 %custom-call.66 = f32[1,128,128]{1,2,0:T(8,128)S(1)} custom-call(f32[1,128,128]{2,1,0:T(8,128)S(1)} %get-tuple-element.44), custom_call_target="InvertDiagBlocksLowerTriangular" | custom-call | tf_op jit(solution)/shard_map/jit(cholesky)/cholesky | solution.py:49
  538.4 2.3 convolution_subtract_fusion.2
  540.7 12.1 %cholesky.485 = f32[128,128]{1,0:T(8,128)S(1)} custom-call(f32[128,128]{1,0:T(8,128)S(1)} %cholesky.591), custom_call_target="Cholesky" | custom-call | tf_op jit(solution)/shard_map/jit(cholesky)/cholesky | solution.py:49
  554.2 9.8 %custom-call.67 = f32[1,128,128]{1,2,0:T(8,128)S(1)} custom-call(f32[1,128,128]{2,1,0:T(8,128)S(1)} %get-tuple-element.41), custom_call_target="InvertDiagBlocksLowerTriangular" | custom-call | tf_op jit(solution)/shard_map/jit(cholesky)/cholesky | solution.py:49
  565.1 2.4 convolution_subtract_fusion.3
  567.5 11.7 %cholesky.504 = f32[128,128]{1,0:T(8,128)S(1)} custom-call(f32[128,128]{1,0:T(8,128)S(1)} %cholesky.596), custom_call_target="Cholesky" | custom-call | tf_op jit(solution)/shard_map/jit(cholesky)/cholesky | solution.py:49
  580.5 9.9 %custom-call.68 = f32[1,128,128]{1,2,0:T(8,128)S(1)} custom-call(f32[1,128,128]{2,1,0:T(8,128)S(1)} %get-tuple-element.38), custom_call_target="InvertDiagBlocksLowerTriangular" | custom-call | tf_op jit(solution)/shard_map/jit(cholesky)/cholesky | solution.py:49
  593.8 11.7 %cholesky.524 = f32[128,128]{1,0:T(8,128)S(1)} custom-call(f32[128,128]{1,0:T(8,128)S(1)} %cholesky.601), custom_call_target="Cholesky" | custom-call | tf_op jit(solution)/shard_map/jit(cholesky)/cholesky | solution.py:49
  606.8 9.8 %custom-call.69 = f32[1,128,128]{1,2,0:T(8,128)S(1)} custom-call(f32[1,128,128]{2,1,0:T(8,128)S(1)} %get-tuple-element.35), custom_call_target="InvertDiagBlocksLowerTriangular" | custom-call | tf_op jit(solution)/shard_map/jit(cholesky)/cholesky | solution.py:49
  619.6 11.9 %cholesky.544 = f32[128,128]{1,0:T(8,128)S(1)} custom-call(f32[128,128]{1,0:T(8,128)S(1)} %cholesky.606), custom_call_target="Cholesky" | custom-call | tf_op jit(solution)/shard_map/jit(cholesky)/cholesky | solution.py:49
  632.9 9.8 %custom-call.70 = f32[1,128,128]{1,2,0:T(8,128)S(1)} custom-call(f32[1,128,128]{2,1,0:T(8,128)S(1)} %get-tuple-element.32), custom_call_target="InvertDiagBlocksLowerTriangular" | custom-call | tf_op jit(solution)/shard_map/jit(cholesky)/cholesky | solution.py:49
  645.3 11.7 %cholesky.562 = f32[128,128]{1,0:T(8,128)S(1)} custom-call(f32[128,128]{1,0:T(8,128)S(1)} %convolution_subtract_fusion.6), custom_call_target="Cholesky" | custom-call | tf_op jit(solution)/shard_map/jit(cholesky)/cholesky | solution.py:49
  664.2 4.9 select_select_fusion
  669.1 23.1 %while.1 = (s32[]{:T(128)}, f32[1024,1024]{1,0:T(8,128)}, s32[8,2]{0,1:T(2,128)S(1)}, f32[8,128,128]{2,1,0:T(8,128)S(1)}, s32[]{:T(128)}) while((s32[]{:T(128)}, f32[1024,1024]{1,0:T(8,128)}, s32[8,2]{0,1:T(2,128)S(1)}, f32[8,128,128]{2,1,0:T(8,128)S(1)}, s32[]{:T(128)}) %tuple.64), condition=%wide.while_cond, body=%wide.while_body.sunk | while | flops 2 | bytes 131181 | solution.py:30
  692.2 78.8 %custom-call.71 = f32[8,128,128]{1,2,0:T(8,128)S(1)} custom-call(f32[8,128,128]{2,1,0:T(8,128)S(1)} %get-tuple-element.12), custom_call_target="InvertDiagBlocksLowerTriangular" | custom-call | tf_op jit(solution)/shard_map/triangular_solve | solution.py:30
  793.5 3.7 fusion.133
  797.8 77.7 %psum.15 = f32[]{:T(128)} all-reduce(f32[]{:T(128)} %multiply_reduce_fusion), channel_id=1, replica_groups=mesh['samp'=64,'par'=4] {'samp','par'}, use_global_device_ids=true, to_apply=%region_22.23 | all-reduce | flops 1 | bytes 8 | tf_op jit(solution)/shard_map/psum | solution.py:52
  (155 shorter events, 81.8 us)
Async XLA Ops:
  6.5 437.2 %all-reduce.4.cloned.1.call-start = ((), (), s32[]{:S(2)}) async-start(), calls=%async_computation.1 | async-start | bytes 8388608 | tf_op jit(solution)/shard_map/psum | solution.py:47
  166.1 2.7 copy-start
  177.0 0.7 copy-start.2
  177.0 1.2 copy-start.4
  177.0 2.6 copy-start.3
  458.5 2.0 copy-start.1
Sparse Core Ops, SparseCore 0:
  177.1 266.5 all-reduce.3
where the time goes:
time: 892 us; the launch traced here: 884 us
  blocking collectives  385 us (43%)
  other arithmetic  271 us (30%)
  waiting for transfers between devices  109 us (12%)
  matrix products  55.6 us (6%)
  local copies, waits for them, and re-layouts  42.4 us (5%)
  between operations  21.4 us (2%)
    another operation x30, other arithmetic, on_device(): factor = jnp.linalg.cholesky(shifted)  173 us
    unnamed x1, blocking collectives  154 us
    all_to_all x1, blocking collectives, on_device(): lax.all_to_all(jacobian, 'samp', split_axis=1, concat_axis=0, tiled=True)  153 us
    psum x1, waiting for transfers between devices, on_device(): gram_total = lax.psum(part_gram, ('samp', 'par'))  109 us
    another operation x3, other arithmetic, solve_both(): lax.linalg.triangular_solve(factor, middle, left_side=True, lower=True, t...  83.8 us
    psum x1, blocking collectives, on_device(): square_sum = lax.psum(jnp.sum(direction * direction), ('samp', 'par'))  77.7 us
    another operation x14, matrix products, on_device(): factor = jnp.linalg.cholesky(shifted)  23.1 us
    another operation x24, local copies, waits for them, and re-layouts  22.9 us
  transfers between devices with their start and end apart: 1, of which 1 were waited for; matrix products, arithmetic and copies ran while one was open for 0% of the time, Pallas kernels for 0%

commit v1 on v0

v1 whole, which is shorter than its diff:
```python
import math

import jax, jax.numpy as jnp
from jax import lax
from jax.experimental import pallas as pl
from jax.experimental.pallas import tpu as pltpu
from jax.sharding import PartitionSpec as P

N = 1024
NB = 128
GR = 8


def split3(x):
    high = x.astype(jnp.bfloat16)
    rest = x - high.astype(jnp.float32)
    mid = rest.astype(jnp.bfloat16)
    low = (rest - mid.astype(jnp.float32)).astype(jnp.bfloat16)
    return high, mid, low


def dot_wide(a, b):
    ah, am, al = split3(a)
    bh, bm, bl = split3(b)
    left = jnp.concatenate([ah, ah, am, am, ah, al], axis=1)
    right = jnp.concatenate([bh, bm, bh, bm, bl, bh], axis=0)
    return jnp.dot(left, right, preferred_element_type=jnp.float32)


def lanes(v, c):
    return jnp.broadcast_to(v[:, c:c + 1], (GR, NB))


def subs(v, r):
    return jnp.broadcast_to(v[r:r + 1, :], (GR, NB))


def invert_block(rows):
    lane = lax.broadcasted_iota(jnp.int32, (GR, NB), 1)
    sub = lax.broadcasted_iota(jnp.int32, (GR, NB), 0)
    count = NB // GR
    for g in range(count):
        base = g * GR
        own = rows[g]
        piv_cols = [lanes(own, base + c) for c in range(GR)]
        in_piv = (lane >= base) & (lane < base + GR)
        row = jnp.where(in_piv, jnp.where(lane - base == sub, 1.0, 0.0), own)
        for q in range(GR):
            at = sub == q
            inv = 1.0 / subs(piv_cols[q], q)
            coef = jnp.where(at, -inv, piv_cols[q] * inv)
            row = jnp.where(at, 0.0, row) - coef * subs(row, q)
            for c in range(q + 1, GR):
                piv_cols[c] = jnp.where(at, 0.0, piv_cols[c]) - coef * subs(piv_cols[c], q)
        spread = [subs(row, q) for q in range(GR)]
        new_rows = []
        for v in range(count):
            if v == g:
                new_rows.append(row)
                continue
            terms = [lanes(rows[v], base + q) * spread[q] for q in range(GR)]
            total = (((terms[0] + terms[1]) + (terms[2] + terms[3]))
                     + ((terms[4] + terms[5]) + (terms[6] + terms[7])))
            new_rows.append(jnp.where(in_piv, 0.0, rows[v]) - total)
        rows = new_rows
    return rows


def solve_kernel(gram_ref, energy_ref, centred_ref, out_ref, work, held, x_row, x_col, sem):
    fetch = pltpu.make_async_copy(centred_ref, held, sem)
    fetch.start()
    sub = lax.broadcasted_iota(jnp.int32, (NB, NB), 0)
    lane = lax.broadcasted_iota(jnp.int32, (NB, NB), 1)
    eye = jnp.where(sub == lane, 1.0, 0.0)
    work[0:N, :] = gram_ref[...]
    for b in range(N // NB):
        at = pl.ds(b * NB, NB)
        work[at, at] = gram_ref[at, at] + 0.5 * eye
    energy = energy_ref[...]
    mean = jnp.sum(energy, axis=1, keepdims=True) * (1.0 / N)
    work[N:N + GR, :] = jnp.broadcast_to(energy - mean, (GR, N))

    def stage(k, carry):
        at = pl.ds(pl.multiple_of(k * NB, NB), NB)
        rows = [work[pl.ds(pl.multiple_of(k * NB + v * GR, GR), GR), at] for v in range(NB // GR)]
        rows = invert_block(rows)
        for v in range(NB // GR):
            work[pl.ds(pl.multiple_of(k * NB + v * GR, GR), GR), at] = rows[v]
        for c in range(N // NB - 1):
            @pl.when(k == c)
            def _():
                own = slice(c * NB, (c + 1) * NB)
                after = slice((c + 1) * NB, N)
                below = slice((c + 1) * NB, N + GR)
                inverse = work[own, own]
                turned = dot_wide(inverse, work[own, after])
                work[below, after] = work[below, after] - dot_wide(work[below, own], turned)
                work[own, after] = turned
        return carry

    lax.fori_loop(0, N // NB, stage, 0)

    for k in range(N // NB - 1, -1, -1):
        own = slice(k * NB, (k + 1) * NB)
        total = work[own, own] * work[N:N + 1, own]
        for j in range(k + 1, N // NB):
            col = slice(j * NB, (j + 1) * NB)
            total = total - work[own, col] * x_row[0:1, col]
        column = jnp.sum(total, axis=1, keepdims=True)
        column = jnp.broadcast_to(column, (NB, NB))
        x_row[0:1, own] = jnp.sum(column * eye, axis=0, keepdims=True)
        x_col[own, :] = column.astype(jnp.bfloat16).astype(jnp.float32)

    weights = x_row[0:1, :].astype(jnp.bfloat16)
    wide = weights.astype(jnp.float32)

    def quad(i, acc):
        at = pl.ds(pl.multiple_of(i * NB, NB), NB)
        part = gram_ref[at, 0:NB] * wide[:, 0:NB]
        for j in range(1, N // NB):
            col = slice(j * NB, (j + 1) * NB)
            part = part + gram_ref[at, col] * wide[:, col]
        return acc + part * x_col[at, :]

    acc = lax.fori_loop(0, N // NB, quad, jnp.zeros((NB, NB), jnp.float32))
    square_sum = jnp.sum(jnp.sum(acc, axis=0, keepdims=True), axis=1, keepdims=True)
    root_mean = jnp.sqrt(jnp.maximum(square_sum, 0.0) / 786432.0 + 1e-06)
    fetch.wait()
    left = jnp.where(lax.broadcasted_iota(jnp.int32, (16, N), 0) == 0, wide, 0.0).astype(jnp.bfloat16)
    direction = jnp.dot(left, held[...], preferred_element_type=jnp.float32)
    out_ref[...] = -direction[0:1, :] / root_mean


def solve_call(gram, energy, centred):
    width = centred.shape[1]
    return pl.pallas_call(
        solve_kernel,
        out_shape=jax.ShapeDtypeStruct((1, width), jnp.float32),
        in_specs=[pl.BlockSpec(memory_space=pltpu.VMEM), pl.BlockSpec(memory_space=pltpu.VMEM), pl.BlockSpec(memory_space=pl.ANY)],
        out_specs=pl.BlockSpec(memory_space=pltpu.VMEM),
        scratch_shapes=[
            pltpu.VMEM((N + GR, N), jnp.float32),
            pltpu.VMEM((N, width), jnp.bfloat16),
            pltpu.VMEM((GR, N), jnp.float32),
            pltpu.VMEM((N, NB), jnp.float32),
            pltpu.SemaphoreType.DMA,
        ],
        compiler_params=pltpu.CompilerParams(vmem_limit_bytes=48 * 1024 * 1024),
        name="solve",
    )(gram, energy, centred)


SITES = 100


def bond_weights():
    side = math.isqrt(SITES)
    site = lax.broadcasted_iota(jnp.int32, (SITES, SITES), 0)
    other = lax.broadcasted_iota(jnp.int32, (SITES, SITES), 1)
    row, col = site // side, site % side
    other_row, other_col = other // side, other % side

    def bond(down, right):
        return ((other_row == (row + down) % side) & (other_col == (col + right) % side)).astype(jnp.float32)

    return 0.25 * (bond(0, 1) + bond(1, 0)) + 0.125 * (bond(1, 1) + bond(1, -1))


def diagonal_energy(spin_bits):
    spin_signs = (2 * spin_bits - 1).astype(jnp.float32)
    return jnp.sum(jnp.dot(spin_signs, bond_weights(), preferred_element_type=jnp.float32) * spin_signs, axis=1)


def on_device(spin_bits, flip_energy, jacobian):
    energy = diagonal_energy(spin_bits) + flip_energy
    first = (lax.axis_index("par") == 0).astype(jnp.float32)
    place = lax.axis_index("samp") * energy.shape[0]
    energy_rows = lax.dynamic_update_slice(jnp.zeros((GR, N), jnp.float32), (energy * first)[None, :], (0, place))
    columns = lax.all_to_all(jacobian, "samp", split_axis=1, concat_axis=0, tiled=True)
    column_mean = jnp.sum(columns, axis=0, dtype=jnp.float32) / N
    centred = (columns.astype(jnp.float32) - column_mean[None, :]).astype(jnp.bfloat16)
    part_gram = lax.dot_general(
        centred, centred, (((1,), (1,)), ((), ())), preferred_element_type=jnp.float32
    )
    total = lax.psum(jnp.concatenate([part_gram, energy_rows], axis=0), ("samp", "par"))
    return solve_call(total[:N], total[N:N + 1], centred).reshape(1, 1, -1)


def solution(mesh):
    return jax.shard_map(
        on_device,
        mesh=mesh,
        in_specs=(P("samp", None), P("samp"), P("samp", "par")),
        out_specs=P("par", "samp", None),
        check_vma=False,
    )
```

time: 892 us -> 508 us (0.57)
  blocking collectives: 385 us -> 0 us
  waiting for transfers between devices: 109 us -> 399 us
  other arithmetic: 271 us -> 17.5 us
  matrix products: 55.6 us -> 7.18 us
  Pallas kernels: 0 us -> 44 us
  local copies, waits for them, and re-layouts: 42.4 us -> 9.86 us
  starting transfers between devices: 0.01 us -> 15.5 us
    another operation x35 -> x0, other arithmetic: 256 us -> none  [the longest x30 173 us: on_device(): factor = jnp.linalg.cholesky(shifted)]
    unnamed x1 -> x0, blocking collectives: 154 us -> none
    all_to_all x1 -> x0, blocking collectives: 153 us -> none  [on_device(): lax.all_to_all(jacobian, 'samp', split_axis=1, concat_axis=0, tiled=True)]
    psum x1, waiting for transfers between devices: 109 us -> 261 us  [on_device(): lax.psum(jnp.concatenate([part_gram, energy_rows], axis=0), ('samp', 'par'))]
    all_to_all x0 -> x1, waiting for transfers between devices: none -> 138 us  [on_device(): lax.all_to_all(jacobian, 'samp', split_axis=1, concat_axis=0, tiled=True)]
    psum x1 -> x0, blocking collectives: 77.7 us -> none  [on_device(): square_sum = lax.psum(jnp.sum(direction * direction), ('samp', 'par'))]
    pallas_call x0 -> x1, Pallas kernels: none -> 44 us  [solve_call(): pl.pallas_call(solve_kernel, out_shape=jax.ShapeDtypeStruct((1, width), j...]
    another operation x44 -> x0, matrix products: 43.6 us -> none  [the longest x14 23.1 us: on_device(): factor = jnp.linalg.cholesky(shifted)]
  transfers between devices with their start and end apart: 1 -> 2, of which waited for: 1 -> 2; matrix products, arithmetic and copies ran while one was open for 0% -> 2% of each run, Pallas kernels for 0% -> 0%
where the time goes in v1:
time: 508 us; the launch traced here: 506 us
  waiting for transfers between devices  399 us (79%)
  Pallas kernels  44 us (9%)
  other arithmetic  17.5 us (3%)
  starting transfers between devices  15.5 us (3%)
  between operations  13.5 us (3%)
  local copies, waits for them, and re-layouts  9.86 us (2%)
  matrix products  7.18 us (1%)
    psum x1, waiting for transfers between devices, on_device(): lax.psum(jnp.concatenate([part_gram, energy_rows], axis=0), ('samp', 'par'))  261 us
    all_to_all x1, waiting for transfers between devices, on_device(): lax.all_to_all(jacobian, 'samp', split_axis=1, concat_axis=0, tiled=True)  138 us
    pallas_call x1, Pallas kernels, solve_call(): pl.pallas_call(solve_kernel, out_shape=jax.ShapeDtypeStruct((1, width), j...  44 us
    all_to_all x1, starting transfers between devices, on_device(): lax.all_to_all(jacobian, 'samp', split_axis=1, concat_axis=0, tiled=True)  15.5 us
    convert_element_type x2, other arithmetic, on_device(): (columns.astype(jnp.float32) - column_mean[None, :]).astype(jnp.bfloat16)  11.5 us
  transfers between devices with their start and end apart: 2, of which 2 were waited for; matrix products, arithmetic and copies ran while one was open for 2% of the time, Pallas kernels for 0%

profile of v1, /device:TPU:1, one launch (start us, length us, event | category | flops | bytes accessed | tf_op | source)
XLA Modules:
  0.0 506.1 jit_solution(14478560218659481430)
XLA Ops:
  6.5 6.1 %copy.7 = bf16[2,64,8,3072]{3,2,0,1:T(8,128)(2,1)} copy(bf16[2,64,8,3072]{3,2,1,0:T(8,128)(2,1)} %bitcast.19) | data formatting | bytes 12582912 | tf_op jit(solution)/shard_map/all_to_all | solution.py:179
  12.6 0.0 copy-start.1
  12.6 0.0 copy-start
  12.6 15.5 %all-to-all-start = ((bf16[16,64,3072]{2,0,1:T(8,128)(2,1)}), bf16[16,64,3072]{2,0,1:T(8,128)(2,1)}, u32[]{:S(2)}, u32[]{:S(2)}) async-start(bf16[16,64,3072]{2,0,1:T(8,128)(2,1)} %bitcast.18), calls=%async_computation | async-start | bytes 12582912 | tf_op jit(solution)/shard_map/all_to_all | solution.py:179
  28.1 0.0 all-reduce.2.cloned.1.call-start
  28.2 0.0 copy-done.1
  28.2 0.5 fusion.1
  28.7 0.0 copy-done
  28.7 0.2 dynamic_update_slice.3
  29.0 137.7 %all-to-all-done = bf16[16,64,3072]{2,0,1:T(8,128)(2,1)} async-done(((bf16[16,64,3072]{2,0,1:T(8,128)(2,1)}), bf16[16,64,3072]{2,0,1:T(8,128)(2,1)}, u32[]{:S(2)}, u32[]{:S(2)}) %all-to-all-start) | async-done | bytes 6291488 | tf_op jit(solution)/shard_map/all_to_all | solution.py:179
  166.7 3.7 convert_reduce_fusion
  170.4 4.4 subtract_convert_fusion
  174.8 6.7 %fusion.70 = f32[1024,1024]{1,0:T(8,128)S(1)} fusion(bf16[1024,3072]{1,0:T(8,128)(2,1)S(1)} %bitcast.20), kind=kOutput, calls=%fused_computation.94 | convolution fusion | flops 6442450944 | bytes 10485760 | tf_op jit(solution)/shard_map/dot_general | solution.py:182
  181.5 2.3 pad_maximum_fusion
  183.7 0.0 all-reduce.2.cloned.1.call-update
  183.8 7.1 %fusion.centred_ref = bf16[1024,3072]{1,0:T(8,128)(2,1)} fusion(f32[3072]{0:T(1024)S(1)} %broadcast_multiply_fusion, bf16[16,64,3072]{2,0,1:T(8,128)(2,1)} %all-to-all-done), kind=kLoop, calls=%fused_computation.1 | loop fusion | flops 9437184 | bytes 12595200 | tf_op jit(solution)/shard_map/convert_element_type | solution.py:181
  190.9 260.9 %all-reduce.2.cloned.1.call-done = f32[1032,1024]{1,0:T(8,128)} async-done(((f32[1032,1024]{1,0:T(8,128)}), f32[1032,1024]{1,0:T(8,128)}) %all-reduce.2.cloned.1.call-update) | async-done | bytes 4227088 | tf_op jit(solution)/shard_map/psum | solution.py:185
  451.7 2.8 slice.8.gram_ref
  454.5 0.8 slice.9.energy_ref
  455.3 44.0 %solve.1 = f32[1,3072]{1,0:T(1,128)} custom-call(f32[1024,1024]{1,0:T(8,128)S(1)} %slice.8.gram_ref, f32[1,1024]{1,0:T(1,128)S(1)} %slice.9.energy_ref, bf16[1024,3072]{1,0:T(8,128)(2,1)} %fusion.centred_ref), custom_call_target="tpu_custom_call" | custom-call | tf_op jit(solution)/shard_map/solve/pallas_call | solution.py:136
  (6 shorter events, 0.0 us)
Async XLA Ops:
  12.6 15.6 %copy-start.1 = (s32[16,100]{1,0:T(8,128)S(1)}, s32[16,100]{1,0:T(8,128)}, u32[]{:S(2)}) copy-start(s32[16,100]{1,0:T(8,128)} %param.3) | copy-start | bytes 19204
  12.6 16.1 %copy-start = (f32[16]{0:T(128)S(1)}, f32[16]{0:T(128)}, u32[]{:S(2)}) copy-start(f32[16]{0:T(128)} %param.4) | copy-start | bytes 196
  12.6 154.0 %all-to-all-start = ((bf16[16,64,3072]{2,0,1:T(8,128)(2,1)}), bf16[16,64,3072]{2,0,1:T(8,128)(2,1)}, u32[]{:S(2)}, u32[]{:S(2)}) async-start(bf16[16,64,3072]{2,0,1:T(8,128)(2,1)} %bitcast.18), calls=%async_computation | async-start | bytes 12582912 | tf_op jit(solution)/shard_map/all_to_all | solution.py:179
  28.1 423.6 %all-reduce.2.cloned.1.call-start = ((), (), s32[]{:S(2)}) async-start(), calls=%async_computation.1 | async-start | bytes 8454144 | tf_op jit(solution)/shard_map/psum | solution.py:185
Sparse Core Ops, SparseCore 0:
  183.9 267.7 all-reduce.1

commit v2 on v1

v2 whole, which is shorter than its diff:
```python
import math

import jax
import jax.numpy as jnp
from jax import lax
from jax.experimental import pallas as pl
from jax.experimental.pallas import tpu as pltpu
from jax.sharding import PartitionSpec as P

SITES = 100
N = 1024
NB = 128
GR = 8
BLOCKS = N // NB
PARAMS = 786432
PER = 16
WIDTH = 3072
PIECES = 4
PIECE = WIDTH // PIECES
PACKED = BLOCKS * (BLOCKS + 1) // 2 * NB
HALF = PACKED // 2
ROWS_ONE = HALF // 4
ROWS_TWO = ROWS_ONE // 4
ROWS_LAST = 16
MESH = pl.DeviceIdType.MESH


def block_at(i, j):
    start = (i * (i + 1) // 2 + j) * NB
    return slice(start, start + NB)


def bond_weights():
    side = math.isqrt(SITES)
    site = lax.broadcasted_iota(jnp.int32, (SITES, SITES), 0)
    other = lax.broadcasted_iota(jnp.int32, (SITES, SITES), 1)
    row, col = site // side, site % side
    other_row, other_col = other // side, other % side

    def bond(down, right):
        hit = (other_row == (row + down) % side) & (other_col == (col + right + side) % side)
        return jnp.where(hit, 1.0, 0.0)

    return 0.25 * (bond(0, 1) + bond(1, 0)) + 0.125 * (bond(1, 1) + bond(1, -1))


def gram_kernel(
    spin_ref, bond_ref, flip_ref, jac_ref,
    gram_ref, energy_ref, centred_ref,
    held, packed, final, tiles, slot_core, slot_one, slot_two, slot_last,
    send_sem, recv_sem, own_sem, tile_send, tile_recv, out_sem, sum_send, sum_recv,
):
    samp, par = lax.axis_index("samp"), lax.axis_index("par")
    core = par % 2
    x_hi, y, z = samp // 32, (samp // 8) % 4, samp % 8
    x = x_hi * 2 + par // 2

    def device(x_at, y_at, z_at, core_at):
        return {"samp": (x_at // 2) * 32 + y_at * 8 + z_at, "par": (x_at % 2) * 2 + core_at}

    barrier = pltpu.get_barrier_semaphore()

    def greet(step, carry):
        pl.semaphore_signal(
            barrier, inc=1, device_id={"samp": lax.rem(samp + step, 64), "par": par}, device_id_type=MESH
        )
        return carry

    lax.fori_loop(1, 64, greet, 0)
    for partner in (device(x, y, z, 1 - core), device((x + 1) % 4, y, z, core), device((x + 3) % 4, y, z, core)):
        pl.semaphore_signal(barrier, inc=1, device_id=partner, device_id_type=MESH)

    mine = pl.ds(pl.multiple_of(samp * PER, PER), PER)
    own = pltpu.make_async_copy(
        jac_ref.at[:, pl.ds(pl.multiple_of(samp * WIDTH, NB), WIDTH)], held.at[mine], own_sem
    )
    own.start()

    signs = (2 * spin_ref[...] - 1).astype(jnp.float32).astype(jnp.bfloat16)
    linked = jnp.dot(signs, bond_ref[...], preferred_element_type=jnp.float32)
    bonds = jnp.sum(linked * signs.astype(jnp.float32), axis=1, keepdims=True)
    values = bonds + flip_ref[...]
    lane = lax.broadcasted_iota(jnp.int32, (PER, NB), 1)
    sample = lax.broadcasted_iota(jnp.int32, (PER, NB), 0)
    line = jnp.sum(jnp.where(lane == sample + (samp % 8) * PER, values, 0.0), axis=0, keepdims=True)
    sub = lax.broadcasted_iota(jnp.int32, (GR, NB), 0)
    tile_at = pl.ds(pl.multiple_of(samp * GR, GR), GR)
    tiles[tile_at, :] = jnp.where(sub == samp // 8, line, 0.0)

    pl.semaphore_wait(barrier, 66)

    def send_tile(step, carry):
        pltpu.make_async_remote_copy(
            src_ref=tiles.at[tile_at],
            dst_ref=tiles.at[tile_at],
            send_sem=tile_send,
            recv_sem=tile_recv,
            device_id={"samp": lax.rem(samp + step, 64), "par": par},
            device_id_type=MESH,
        ).start()
        return carry

    def send_block(piece, x_to, y_to, z_to):
        to = x_to * 32 + y_to * 8 + z_to
        pltpu.make_async_remote_copy(
            src_ref=jac_ref.at[:, pl.ds(pl.multiple_of(to * WIDTH + piece * PIECE, NB), PIECE)],
            dst_ref=held.at[mine, pl.ds(pl.multiple_of(piece * PIECE, NB), PIECE)],
            send_sem=send_sem,
            recv_sem=recv_sem.at[piece],
            device_id={"samp": to, "par": par},
            device_id_type=MESH,
        ).start()

    def send_plane(step, carry):
        piece, plane = step // 8, step % 8
        x_to = (x_hi + 1 - plane // 4) % 2
        y_to = (y + 6 - plane % 4) % 4
        for z_off in (4, 7, 3, 5, 2, 6, 1):
            send_block(piece, x_to, y_to, (z + z_off) % 8)

        @pl.when(plane != 6)
        def _():
            send_block(piece, x_to, y_to, z)

        return carry

    lax.fori_loop(0, 8 * PIECES, send_plane, 0)
    lax.fori_loop(1, 64, send_tile, 0)
    own.wait()
    packed[...] = jnp.zeros_like(packed)

    def work_piece(piece, carry):
        cols = pl.ds(pl.multiple_of(piece * PIECE, NB), PIECE)
        others = held.at[pl.ds(0, N - PER), cols]
        pltpu.make_async_copy(others, others, recv_sem.at[piece]).wait()

        def add_rows(i, total):
            return total + held[pl.ds(pl.multiple_of(i * PER, PER), PER), cols].astype(jnp.float32)

        total = lax.fori_loop(0, N // PER, add_rows, jnp.zeros((PER, PIECE), jnp.float32), unroll=4)
        mean = jnp.sum(total, axis=0, keepdims=True) * (1.0 / N)

        def centre_rows(i, carry):
            at = pl.ds(pl.multiple_of(i * PER, PER), PER)
            held[at, cols] = (held[at, cols].astype(jnp.float32) - mean).astype(jnp.bfloat16)
            return carry

        lax.fori_loop(0, N // PER, centre_rows, 0, unroll=4)
        pltpu.make_async_copy(held.at[:, cols], centred_ref.at[:, cols], out_sem.at[piece]).start()
        for i in range(0, BLOCKS, 2):
            size = (i + 2) * NB
            product = lax.dot_general(
                held[i * NB:size, cols], held[0:size, cols], (((1,), (1,)), ((), ())),
                preferred_element_type=jnp.float32,
            )
            for r in range(2):
                for j in range(i + r + 1):
                    at = block_at(i + r, j)
                    packed[at, :] = packed[at, :] + product[r * NB:(r + 1) * NB, j * NB:(j + 1) * NB]
        return carry

    lax.fori_loop(0, PIECES, work_piece, 0)

    x_or_y = (x, y)
    pos_one = x_or_y[0] + core * (y - x)
    pos_two = x_or_y[1] + core * (x - y)

    def on_one(at):
        return device(at + core * (x - at), y + core * (at - y), z, core)

    def on_two(at):
        return device(x + core * (at - x), at + core * (y - at), z, core)

    def rows(start, size):
        return pl.ds(pl.multiple_of(start, GR), size)

    def send(stage, source, target, to):
        pltpu.make_async_remote_copy(
            src_ref=source, dst_ref=target, send_sem=sum_send.at[stage], recv_sem=sum_recv.at[stage],
            device_id=to, device_id_type=MESH,
        ).start()

    def arrived(stage, like):
        pltpu.make_async_copy(like, like, sum_recv.at[stage]).wait()

    def left(stage, like):
        pltpu.make_async_copy(like, like, sum_send.at[stage]).wait()

    half = core * HALF
    send(0, packed.at[rows((1 - core) * HALF, HALF)], slot_core, device(x, y, z, 1 - core))
    arrived(0, slot_core)
    packed[rows(half, HALF), :] = packed[rows(half, HALF), :] + slot_core[...]

    for step in (2, 1, 3):
        to = (pos_one + step) % 4
        send(1, packed.at[rows(half + to * ROWS_ONE, ROWS_ONE)], slot_one.at[pos_one], on_one(to))
    arrived(1, slot_one.at[pl.ds(0, 3)])
    one = half + pos_one * ROWS_ONE
    packed[rows(one, ROWS_ONE), :] = (packed[rows(one, ROWS_ONE), :] + slot_one[(pos_one + 1) % 4]) + (
        slot_one[(pos_one + 2) % 4] + slot_one[(pos_one + 3) % 4]
    )

    for step in (2, 1, 3):
        to = (pos_two + step) % 4
        send(2, packed.at[rows(one + to * ROWS_TWO, ROWS_TWO)], slot_two.at[pos_two], on_two(to))
    arrived(2, slot_two.at[pl.ds(0, 3)])
    two = one + pos_two * ROWS_TWO
    packed[rows(two, ROWS_TWO), :] = (packed[rows(two, ROWS_TWO), :] + slot_two[(pos_two + 1) % 4]) + (
        slot_two[(pos_two + 2) % 4] + slot_two[(pos_two + 3) % 4]
    )

    spare = rows(two + 8 * ROWS_LAST, ROWS_LAST)
    for step in (4, 3, 5, 2, 6, 1, 7):
        to = (z + step) % 8
        send(3, packed.at[rows(two + to * ROWS_LAST, ROWS_LAST)], slot_last.at[z, 0:ROWS_LAST], device(x, y, to, core))
        send(3, packed.at[spare], slot_last.at[z, ROWS_LAST:2 * ROWS_LAST], device(x, y, to, core))
    last = rows(two + z * ROWS_LAST, ROWS_LAST)
    slot_last[z, 0:ROWS_LAST] = packed[last, :]
    slot_last[z, ROWS_LAST:2 * ROWS_LAST] = packed[spare, :]
    arrived(3, slot_last.at[pl.ds(0, 7)])
    total = slot_last[0]
    for i in range(1, 8):
        total = total + slot_last[i]
    final[last, :] = total[0:ROWS_LAST]
    final[spare, :] = total[ROWS_LAST:2 * ROWS_LAST]

    for step in (4, 3, 5, 2, 6, 1, 7):
        send(4, final.at[last], final.at[last], device(x, y, (z + step) % 8, core))
    arrived(4, final.at[pl.ds(0, 7 * ROWS_LAST)])
    part = rows(two, ROWS_TWO)
    for step in (2, 1, 3):
        send(5, final.at[part], final.at[part], on_two((pos_two + step) % 4))
    arrived(5, final.at[pl.ds(0, 3 * ROWS_TWO)])
    part = rows(one, ROWS_ONE)
    for step in (2, 1, 3):
        send(6, final.at[part], final.at[part], on_one((pos_one + step) % 4))
    arrived(6, final.at[pl.ds(0, 3 * ROWS_ONE)])
    part = rows(half, HALF)
    send(7, final.at[part], final.at[part], device(x, y, z, 1 - core))

    others = tiles.at[pl.ds(0, 63 * GR)]
    pltpu.make_async_copy(others, others, tile_recv).wait()
    energy = tiles[0:GR, :]
    for i in range(1, 64):
        energy = energy + tiles[i * GR:(i + 1) * GR, :]
    energy_ref[...] = energy

    arrived(7, final.at[pl.ds(0, HALF)])
    result = pltpu.make_async_copy(final, gram_ref, own_sem)
    result.start()

    for piece in range(PIECES):
        cols = pl.ds(piece * PIECE, PIECE)
        pltpu.make_async_copy(held.at[:, cols], centred_ref.at[:, cols], out_sem.at[piece]).wait()
    others = held.at[pl.ds(0, N - PER)]
    pltpu.make_async_copy(others, others, send_sem).wait()
    others = tiles.at[pl.ds(0, 63 * GR)]
    pltpu.make_async_copy(others, others, tile_send).wait()
    left(0, slot_core)
    left(1, slot_one.at[pl.ds(0, 3)])
    left(2, slot_two.at[pl.ds(0, 3)])
    left(3, slot_last.at[pl.ds(0, 7)])
    left(4, final.at[pl.ds(0, 7 * ROWS_LAST)])
    left(5, final.at[pl.ds(0, 3 * ROWS_TWO)])
    left(6, final.at[pl.ds(0, 3 * ROWS_ONE)])
    left(7, final.at[pl.ds(0, HALF)])
    result.wait()


def gram_call(spin_bits, flip_energy, jacobian):
    vmem = pl.BlockSpec(memory_space=pltpu.VMEM)
    anywhere = pl.BlockSpec(memory_space=pl.ANY)
    return pl.pallas_call(
        gram_kernel,
        out_shape=(
            jax.ShapeDtypeStruct((PACKED, NB), jnp.float32),
            jax.ShapeDtypeStruct((GR, NB), jnp.float32),
            jax.ShapeDtypeStruct((N, WIDTH), jnp.bfloat16),
        ),
        in_specs=[vmem, vmem, vmem, anywhere],
        out_specs=(anywhere, vmem, anywhere),
        scratch_shapes=[
            pltpu.VMEM((N, WIDTH), jnp.bfloat16),
            pltpu.VMEM((PACKED, NB), jnp.float32),
            pltpu.VMEM((PACKED, NB), jnp.float32),
            pltpu.VMEM((64 * GR, NB), jnp.float32),
            pltpu.VMEM((HALF, NB), jnp.float32),
            pltpu.VMEM((4, ROWS_ONE, NB), jnp.float32),
            pltpu.VMEM((4, ROWS_TWO, NB), jnp.float32),
            pltpu.VMEM((8, 2 * ROWS_LAST, NB), jnp.float32),
            pltpu.SemaphoreType.DMA,
            pltpu.SemaphoreType.DMA((PIECES,)),
            pltpu.SemaphoreType.DMA,
            pltpu.SemaphoreType.DMA,
            pltpu.SemaphoreType.DMA,
            pltpu.SemaphoreType.DMA((PIECES,)),
            pltpu.SemaphoreType.DMA((8,)),
            pltpu.SemaphoreType.DMA((8,)),
        ],
        compiler_params=pltpu.CompilerParams(
            collective_id=0, has_side_effects=True, vmem_limit_bytes=48 * 1024 * 1024
        ),
        name="gram",
    )(spin_bits, bond_weights().astype(jnp.bfloat16), flip_energy.reshape(PER, 1), jacobian)


def split3(x):
    high = x.astype(jnp.bfloat16)
    rest = x - high.astype(jnp.float32)
    mid = rest.astype(jnp.bfloat16)
    low = (rest - mid.astype(jnp.float32)).astype(jnp.bfloat16)
    return high, mid, low


def dot_wide(a, b, turned=False):
    ah, am, al = split3(a)
    bh, bm, bl = split3(b)
    left = jnp.concatenate([ah, ah, am, am, ah, al], axis=1)
    right = jnp.concatenate([bh, bm, bh, bm, bl, bh], axis=1 if turned else 0)
    dims = (((1,), (1 if turned else 0,)), ((), ()))
    return lax.dot_general(left, right, dims, preferred_element_type=jnp.float32)


def lanes(v, c):
    return jnp.broadcast_to(v[:, c:c + 1], (GR, NB))


def subs(v, r):
    return jnp.broadcast_to(v[r:r + 1, :], (GR, NB))


def invert_block(rows):
    lane = lax.broadcasted_iota(jnp.int32, (GR, NB), 1)
    sub = lax.broadcasted_iota(jnp.int32, (GR, NB), 0)
    count = NB // GR
    for g in range(count):
        base = g * GR
        own = rows[g]
        piv_cols = [lanes(own, base + c) for c in range(GR)]
        in_piv = (lane >= base) & (lane < base + GR)
        row = jnp.where(in_piv, jnp.where(lane - base == sub, 1.0, 0.0), own)
        for q in range(GR):
            at = sub == q
            inv = 1.0 / subs(piv_cols[q], q)
            coef = jnp.where(at, -inv, piv_cols[q] * inv)
            row = jnp.where(at, 0.0, row) - coef * subs(row, q)
            for c in range(q + 1, GR):
                piv_cols[c] = jnp.where(at, 0.0, piv_cols[c]) - coef * subs(piv_cols[c], q)
        spread = [subs(row, q) for q in range(GR)]
        new_rows = []
        for v in range(count):
            if v == g:
                new_rows.append(row)
                continue
            terms = [lanes(rows[v], base + q) * spread[q] for q in range(GR)]
            total = (((terms[0] + terms[1]) + (terms[2] + terms[3]))
                     + ((terms[4] + terms[5]) + (terms[6] + terms[7])))
            new_rows.append(jnp.where(in_piv, 0.0, rows[v]) - total)
        rows = new_rows
    return rows


def solve_kernel(gram_ref, energy_ref, centred_ref, out_ref, work, held, x_row, x_col, sem):
    fetch = pltpu.make_async_copy(centred_ref, held, sem)
    fetch.start()
    sub = lax.broadcasted_iota(jnp.int32, (NB, NB), 0)
    lane = lax.broadcasted_iota(jnp.int32, (NB, NB), 1)
    eye = jnp.where(sub == lane, 1.0, 0.0)
    for i in range(BLOCKS):
        at = slice(i * NB, (i + 1) * NB)
        for j in range(i):
            work[at, j * NB:(j + 1) * NB] = gram_ref[block_at(i, j), :]
        work[at, at] = gram_ref[block_at(i, i), :] + 0.5 * eye
    tile = energy_ref[...]
    mean = jnp.sum(jnp.sum(tile, axis=1, keepdims=True), axis=0, keepdims=True) * (1.0 / N)
    tile = tile - mean
    for i in range(BLOCKS):
        work[N:N + GR, i * NB:(i + 1) * NB] = subs(tile, i)

    def stage(k, carry):
        at = pl.ds(pl.multiple_of(k * NB, NB), NB)
        rows = [work[pl.ds(pl.multiple_of(k * NB + v * GR, GR), GR), at] for v in range(NB // GR)]
        rows = invert_block(rows)
        for v in range(NB // GR):
            work[pl.ds(pl.multiple_of(k * NB + v * GR, GR), GR), at] = rows[v]
        for c in range(BLOCKS - 1):
            @pl.when(k == c)
            def _():
                own = slice(c * NB, (c + 1) * NB)
                after = slice((c + 1) * NB, N)
                below = slice((c + 1) * NB, N + GR)
                turned = dot_wide(work[own, own], work[after, own], turned=True)
                work[below, after] = work[below, after] - dot_wide(work[below, own], turned)
                work[own, after] = turned
        return carry

    lax.fori_loop(0, BLOCKS, stage, 0)

    for k in range(BLOCKS - 1, -1, -1):
        own = slice(k * NB, (k + 1) * NB)
        total = work[own, own] * work[N:N + 1, own]
        for j in range(k + 1, BLOCKS):
            col = slice(j * NB, (j + 1) * NB)
            total = total - work[own, col] * x_row[0:1, col]
        column = jnp.sum(total, axis=1, keepdims=True)
        column = jnp.broadcast_to(column, (NB, NB))
        x_row[0:1, own] = jnp.sum(column * eye, axis=0, keepdims=True)
        x_col[own, :] = column.astype(jnp.bfloat16).astype(jnp.float32)

    wide = x_row[0:1, :].astype(jnp.bfloat16).astype(jnp.float32)

    acc = jnp.zeros((NB, NB), jnp.float32)
    for i in range(BLOCKS):
        part = gram_ref[block_at(i, i), :] * (0.5 * wide[:, i * NB:(i + 1) * NB])
        for j in range(i):
            part = part + gram_ref[block_at(i, j), :] * wide[:, j * NB:(j + 1) * NB]
        acc = acc + part * x_col[i * NB:(i + 1) * NB, :]
    square_sum = 2.0 * jnp.sum(jnp.sum(acc, axis=0, keepdims=True), axis=1, keepdims=True)
    root_mean = jnp.sqrt(jnp.maximum(square_sum, 0.0) / PARAMS + 1e-06)
    fetch.wait()
    left = jnp.where(lax.broadcasted_iota(jnp.int32, (PER, N), 0) == 0, wide, 0.0).astype(jnp.bfloat16)
    direction = jnp.dot(left, held[...], preferred_element_type=jnp.float32)
    out_ref[...] = -direction[0:1, :] / root_mean


def solve_call(gram, energy, centred):
    vmem = pl.BlockSpec(memory_space=pltpu.VMEM)
    return pl.pallas_call(
        solve_kernel,
        out_shape=jax.ShapeDtypeStruct((1, WIDTH), jnp.float32),
        in_specs=[vmem, vmem, pl.BlockSpec(memory_space=pl.ANY)],
        out_specs=vmem,
        scratch_shapes=[
            pltpu.VMEM((N + GR, N), jnp.float32),
            pltpu.VMEM((N, WIDTH), jnp.bfloat16),
            pltpu.VMEM((GR, N), jnp.float32),
            pltpu.VMEM((N, NB), jnp.float32),
            pltpu.SemaphoreType.DMA,
        ],
        compiler_params=pltpu.CompilerParams(vmem_limit_bytes=48 * 1024 * 1024),
        name="solve",
    )(gram, energy, centred)


def on_device(spin_bits, flip_energy, jacobian):
    gram, energy, centred = gram_call(spin_bits, flip_energy, jacobian)
    return solve_call(gram, energy, centred).reshape(1, 1, -1)


def solution(mesh):
    return jax.shard_map(
        on_device,
        mesh=mesh,
        in_specs=(P("samp", None), P("samp"), P("samp", "par")),
        out_specs=P("par", "samp", None),
        check_vma=False,
    )
```

time: 508 us -> 244 us (0.48)
  waiting for transfers between devices: 399 us -> 0 us
  Pallas kernels: 44 us -> 242 us
  other arithmetic: 17.5 us -> 0.3 us
  starting transfers between devices: 15.5 us -> 0 us
  between operations: 13.5 us -> 0.03 us
  local copies, waits for them, and re-layouts: 9.86 us -> 1.43 us
  matrix products: 7.18 us -> 0 us
    psum x1 -> x0, waiting for transfers between devices: 261 us -> none  [on_device(): lax.psum(jnp.concatenate([part_gram, energy_rows], axis=0), ('samp', 'par'))]
    pallas_call x1 -> x2, Pallas kernels: 44 us -> 242 us  [the longest x1 197 us: gram_call(): pl.pallas_call(gram_kernel, out_shape=(jax.ShapeDtypeStruct((PACKED, NB),...]
    all_to_all x1 -> x0, waiting for transfers between devices: 138 us -> none  [on_device(): lax.all_to_all(jacobian, 'samp', split_axis=1, concat_axis=0, tiled=True)]
    all_to_all x1 -> x0, starting transfers between devices: 15.5 us -> none  [on_device(): lax.all_to_all(jacobian, 'samp', split_axis=1, concat_axis=0, tiled=True)]
    convert_element_type x2 -> x1, other arithmetic: 11.5 us -> 0.27 us  [gram_call(): bond_weights().astype(jnp.bfloat16)]
    dot_general x2 -> x0, matrix products: 7.18 us -> none  [the longest x1 6.69 us: on_device(): lax.dot_general(centred, centred, (((1,), (1,)), ((), ())), preferred_ele...]
    all_to_all x1 -> x0, local copies, waits for them, and re-layouts: 6.08 us -> none  [on_device(): lax.all_to_all(jacobian, 'samp', split_axis=1, concat_axis=0, tiled=True)]
  transfers between devices with their start and end apart: 2 -> 0, of which waited for: 2 -> 0; matrix products, arithmetic and copies ran while one was open for 2% -> 0% of each run, Pallas kernels for 0% -> 0%
where the time goes in v2:
time: 244 us
  Pallas kernels  242 us (99%)
    pallas_call x1, Pallas kernels, gram_call(): pl.pallas_call(gram_kernel, out_shape=(jax.ShapeDtypeStruct((PACKED, NB),...  197 us
    pallas_call x1, Pallas kernels, solve_call(): pl.pallas_call(solve_kernel, out_shape=jax.ShapeDtypeStruct((1, WIDTH), j...  44.6 us

profile of v2, /device:TPU:1, one launch (start us, length us, event | category | flops | bytes accessed | tf_op | source)
XLA Modules:
  0.0 243.7 jit_solution(2313444565436416158)
XLA Ops:
  0.0 0.7 copy.4.flip_ref
  0.8 0.3 add_convert_fusion.bond_ref
  1.0 0.0 copy-start
  1.1 0.7 copy-done
  1.7 197.3 %gram.1 = (f32[4608,128]{1,0:T(8,128)S(1)}, f32[8,128]{1,0:T(8,128)S(1)}, bf16[1024,3072]{1,0:T(8,128)(2,1)}) custom-call(s32[16,100]{1,0:T(8,128)S(1)} %copy-done, bf16[100,100]{1,0:T(8,128)(2,1)S(1)} %add_convert_fusion.bond_ref, f32[16,1]{1,0:T(8,128)S(1)} %copy.4.flip_ref, bf16[16,196608]{1,0:T(8,128)(2,1)} %jac_ref.1), custom_call_target="tpu_custom_call" | custom-call | tf_op jit(solution)/shard_map/gram/pallas_call | solution.py:273
  199.1 44.6 %solve.1 = f32[1,3072]{1,0:T(1,128)} custom-call(f32[4608,128]{1,0:T(8,128)S(1)} %get-tuple-element.8.gram_ref, f32[8,128]{1,0:T(8,128)S(1)} %get-tuple-element.9.energy_ref, bf16[1024,3072]{1,0:T(8,128)(2,1)} %get-tuple-element.10.centred_ref), custom_call_target="tpu_custom_call" | custom-call | tf_op jit(solution)/shard_map/solve/pallas_call | solution.py:428
  (3 shorter events, 0.0 us)
Async XLA Ops:
  1.0 0.7 copy-start

commit v3 on v2

--- a/solution.py
+++ b/solution.py
@@ -19,14 +19,16 @@
 PIECE = WIDTH // PIECES
 PACKED = BLOCKS * (BLOCKS + 1) // 2 * NB
 HALF = PACKED // 2
-ROWS_ONE = HALF // 4
+ROWS_CORE = HALF // 2
+ROWS_ONE = ROWS_CORE // 4
 ROWS_TWO = ROWS_ONE // 4
-ROWS_LAST = 16
+ROWS_LAST = 8
+STEPS = 8
 MESH = pl.DeviceIdType.MESH
 
 
 def block_at(i, j):
-    start = (i * (i + 1) // 2 + j) * NB
+    start = (j * BLOCKS - j * (j - 1) // 2 + i - j) * NB
     return slice(start, start + NB)
 
 
@@ -34,20 +36,151 @@
     side = math.isqrt(SITES)
     site = lax.broadcasted_iota(jnp.int32, (SITES, SITES), 0)
     other = lax.broadcasted_iota(jnp.int32, (SITES, SITES), 1)
-    row, col = site // side, site % side
-    other_row, other_col = other // side, other % side
+    row = (site * 205) >> 11
+    col = site - row * side
 
     def bond(down, right):
-        hit = (other_row == (row + down) % side) & (other_col == (col + right + side) % side)
-        return jnp.where(hit, 1.0, 0.0)
+        to_row, to_col = row + down, col + right
+        to_row = jnp.where(to_row >= side, to_row - side, to_row)
+        to_col = jnp.where(to_col >= side, to_col - side, jnp.where(to_col < 0, to_col + side, to_col))
+        return jnp.where(other == to_row * side + to_col, 1.0, 0.0)
 
     return 0.25 * (bond(0, 1) + bond(1, 0)) + 0.125 * (bond(1, 1) + bond(1, -1))
 
 
+def sum_blocks(place, device, packed, final, slots, sum_send, sum_recv):
+    x, y, z, core = place
+    slot_core, slot_one, slot_two, slot_last, staged = slots
+    pos_one = x + core * (y - x)
+    pos_two = y + core * (x - y)
+    other_core = device(x, y, z, 1 - core)
+
+    def on_one(at):
+        return device(at + core * (x - at), y + core * (at - y), z, core)
+
+    def on_two(at):
+        return device(x + core * (at - x), at + core * (y - at), z, core)
+
+    def rows(start, size):
+        return pl.ds(pl.multiple_of(start, GR), size)
+
+    def send(part, step, source, target, to):
+        at = part * STEPS + step
+        pltpu.make_async_remote_copy(
+            src_ref=source, dst_ref=target, send_sem=sum_send.at[at], recv_sem=sum_recv.at[at],
+            device_id=to, device_id_type=MESH,
+        ).start()
+
+    def likes(part):
+        return (
+            slot_core.at[part],
+            slot_one.at[part, pl.ds(0, 3)],
+            slot_two.at[part, pl.ds(0, 3)],
+            slot_last.at[part, pl.ds(0, 7)],
+            final.at[pl.ds(0, 7 * ROWS_LAST)],
+            final.at[pl.ds(0, 3 * ROWS_TWO)],
+            final.at[pl.ds(0, 3 * ROWS_ONE)],
+            final.at[pl.ds(0, ROWS_CORE)],
+        )
+
+    def arrived(part, step):
+        like = likes(part)[step]
+        pltpu.make_async_copy(like, like, sum_recv.at[part * STEPS + step]).wait()
+
+    def starts(part):
+        half = part * HALF + core * ROWS_CORE
+        one = half + pos_one * ROWS_ONE
+        return half, one, one + pos_two * ROWS_TWO
+
+    def to_core(part):
+        source = packed.at[rows(part * HALF + (1 - core) * ROWS_CORE, ROWS_CORE)]
+        send(part, 0, source, slot_core.at[part], other_core)
+
+    def to_one(part):
+        half, one, two = starts(part)
+        arrived(part, 0)
+        packed[rows(half, ROWS_CORE), :] = packed[rows(half, ROWS_CORE), :] + slot_core[part]
+        for step in (2, 1, 3):
+            to = (pos_one + step) % 4
+            send(part, 1, packed.at[rows(half + to * ROWS_ONE, ROWS_ONE)], slot_one.at[part, pos_one], on_one(to))
+
+    def add_three(start, size, slot, part, pos):
+        at = rows(start, size)
+        packed[at, :] = (packed[at, :] + slot[part, (pos + 1) % 4]) + (
+            slot[part, (pos + 2) % 4] + slot[part, (pos + 3) % 4]
+        )
+
+    def to_two(part):
+        half, one, two = starts(part)
+        arrived(part, 1)
+        add_three(one, ROWS_ONE, slot_one, part, pos_one)
+        for step in (2, 1, 3):
+            to = (pos_two + step) % 4
+            send(part, 2, packed.at[rows(one + to * ROWS_TWO, ROWS_TWO)], slot_two.at[part, pos_two], on_two(to))
+
+    def to_last(part):
+        half, one, two = starts(part)
+        arrived(part, 2)
+        add_three(two, ROWS_TWO, slot_two, part, pos_two)
+        spare = packed[rows(two + 8 * ROWS_LAST, ROWS_LAST), :]
+        for i in range(8):
+            staged[part, i, 0:ROWS_LAST] = packed[rows(two + i * ROWS_LAST, ROWS_LAST), :]
+            staged[part, i, ROWS_LAST:2 * ROWS_LAST] = spare
+        for step in (4, 3, 5, 2, 6, 1, 7):
+            to = (z + step) % 8
+            send(part, 3, staged.at[part, to], slot_last.at[part, z], device(x, y, to, core))
+
+    def back_last(part):
+        half, one, two = starts(part)
+        slot_last[part, z] = staged[part, z]
+        arrived(part, 3)
+        total = slot_last[part, 0]
+        for i in range(1, 8):
+            total = total + slot_last[part, i]
+        last = rows(two + z * ROWS_LAST, ROWS_LAST)
+        final[last, :] = total[0:ROWS_LAST]
+        final[rows(two + 8 * ROWS_LAST, ROWS_LAST), :] = total[ROWS_LAST:2 * ROWS_LAST]
+        for step in (4, 3, 5, 2, 6, 1, 7):
+            send(part, 4, final.at[last], final.at[last], device(x, y, (z + step) % 8, core))
+
+    def back_two(part):
+        half, one, two = starts(part)
+        arrived(part, 4)
+        for step in (2, 1, 3):
+            own = final.at[rows(two, ROWS_TWO)]
+            send(part, 5, own, own, on_two((pos_two + step) % 4))
+
+    def back_one(part):
+        half, one, two = starts(part)
+        arrived(part, 5)
+        for step in (2, 1, 3):
+            own = final.at[rows(one, ROWS_ONE)]
+            send(part, 6, own, own, on_one((pos_one + step) % 4))
+
+    def back_core(part):
+        half, one, two = starts(part)
+        arrived(part, 6)
+        own = final.at[rows(half, ROWS_CORE)]
+        send(part, 7, own, own, other_core)
+
+    for move in (to_core, to_one, to_two, to_last, back_last, back_two, back_one, back_core):
+        for part in range(2):
+            move(part)
+
+    def finish():
+        for part in range(2):
+            arrived(part, 7)
+            for step in range(STEPS):
+                like = likes(part)[step]
+                pltpu.make_async_copy(like, like, sum_send.at[part * STEPS + step]).wait()
+
+    return finish
+
+
 def gram_kernel(
-    spin_ref, bond_ref, flip_ref, jac_ref,
+    spin_ref, flip_ref, jac_ref,
     gram_ref, energy_ref, centred_ref,
-    held, packed, final, tiles, slot_core, slot_one, slot_two, slot_last,
+    held, packed, final, tiles, slot_core, slot_one, slot_two, slot_last, staged,
     send_sem, recv_sem, own_sem, tile_send, tile_recv, out_sem, sum_send, sum_recv,
 ):
     samp, par = lax.axis_index("samp"), lax.axis_index("par")
@@ -77,9 +210,11 @@
     own.start()
 
     signs = (2 * spin_ref[...] - 1).astype(jnp.float32).astype(jnp.bfloat16)
-    linked = jnp.dot(signs, bond_ref[...], preferred_element_type=jnp.float32)
+    linked = jnp.dot(signs, bond_weights().astype(jnp.bfloat16), preferred_element_type=jnp.float32)
     bonds = jnp.sum(linked * signs.astype(jnp.float32), axis=1, keepdims=True)
-    values = bonds + flip_ref[...]
+    square = (PER, PER)
+    same = lax.broadcasted_iota(jnp.int32, square, 0) == lax.broadcasted_iota(jnp.int32, square, 1)
+    values = bonds + jnp.sum(jnp.where(same, flip_ref[...], 0.0), axis=1, keepdims=True)
     lane = lax.broadcasted_iota(jnp.int32, (PER, NB), 1)
     sample = lax.broadcasted_iota(jnp.int32, (PER, NB), 0)
     line = jnp.sum(jnp.where(lane == sample + (samp % 8) * PER, values, 0.0), axis=0, keepdims=True)
@@ -161,82 +296,8 @@
 
     lax.fori_loop(0, PIECES, work_piece, 0)
 
-    x_or_y = (x, y)
-    pos_one = x_or_y[0] + core * (y - x)
-    pos_two = x_or_y[1] + core * (x - y)
-
-    def on_one(at):
-        return device(at + core * (x - at), y + core * (at - y), z, core)
-
-    def on_two(at):
-        return device(x + core * (at - x), at + core * (y - at), z, core)
-
-    def rows(start, size):
-        return pl.ds(pl.multiple_of(start, GR), size)
-
-    def send(stage, source, target, to):
-        pltpu.make_async_remote_copy(
-            src_ref=source, dst_ref=target, send_sem=sum_send.at[stage], recv_sem=sum_recv.at[stage],
-            device_id=to, device_id_type=MESH,
-        ).start()
-
-    def arrived(stage, like):
-        pltpu.make_async_copy(like, like, sum_recv.at[stage]).wait()
-
-    def left(stage, like):
-        pltpu.make_async_copy(like, like, sum_send.at[stage]).wait()
-
-    half = core * HALF
-    send(0, packed.at[rows((1 - core) * HALF, HALF)], slot_core, device(x, y, z, 1 - core))
-    arrived(0, slot_core)
-    packed[rows(half, HALF), :] = packed[rows(half, HALF), :] + slot_core[...]
-
-    for step in (2, 1, 3):
-        to = (pos_one + step) % 4
-        send(1, packed.at[rows(half + to * ROWS_ONE, ROWS_ONE)], slot_one.at[pos_one], on_one(to))
-    arrived(1, slot_one.at[pl.ds(0, 3)])
-    one = half + pos_one * ROWS_ONE
-    packed[rows(one, ROWS_ONE), :] = (packed[rows(one, ROWS_ONE), :] + slot_one[(pos_one + 1) % 4]) + (
-        slot_one[(pos_one + 2) % 4] + slot_one[(pos_one + 3) % 4]
-    )
-
-    for step in (2, 1, 3):
-        to = (pos_two + step) % 4
-        send(2, packed.at[rows(one + to * ROWS_TWO, ROWS_TWO)], slot_two.at[pos_two], on_two(to))
-    arrived(2, slot_two.at[pl.ds(0, 3)])
-    two = one + pos_two * ROWS_TWO
-    packed[rows(two, ROWS_TWO), :] = (packed[rows(two, ROWS_TWO), :] + slot_two[(pos_two + 1) % 4]) + (
-        slot_two[(pos_two + 2) % 4] + slot_two[(pos_two + 3) % 4]
-    )
-
-    spare = rows(two + 8 * ROWS_LAST, ROWS_LAST)
-    for step in (4, 3, 5, 2, 6, 1, 7):
-        to = (z + step) % 8
-        send(3, packed.at[rows(two + to * ROWS_LAST, ROWS_LAST)], slot_last.at[z, 0:ROWS_LAST], device(x, y, to, core))
-        send(3, packed.at[spare], slot_last.at[z, ROWS_LAST:2 * ROWS_LAST], device(x, y, to, core))
-    last = rows(two + z * ROWS_LAST, ROWS_LAST)
-    slot_last[z, 0:ROWS_LAST] = packed[last, :]
-    slot_last[z, ROWS_LAST:2 * ROWS_LAST] = packed[spare, :]
-    arrived(3, slot_last.at[pl.ds(0, 7)])
-    total = slot_last[0]
-    for i in range(1, 8):
-        total = total + slot_last[i]
-    final[last, :] = total[0:ROWS_LAST]
-    final[spare, :] = total[ROWS_LAST:2 * ROWS_LAST]
-
-    for step in (4, 3, 5, 2, 6, 1, 7):
-        send(4, final.at[last], final.at[last], device(x, y, (z + step) % 8, core))
-    arrived(4, final.at[pl.ds(0, 7 * ROWS_LAST)])
-    part = rows(two, ROWS_TWO)
-    for step in (2, 1, 3):
-        send(5, final.at[part], final.at[part], on_two((pos_two + step) % 4))
-    arrived(5, final.at[pl.ds(0, 3 * ROWS_TWO)])
-    part = rows(one, ROWS_ONE)
-    for step in (2, 1, 3):
-        send(6, final.at[part], final.at[part], on_one((pos_one + step) % 4))
-    arrived(6, final.at[pl.ds(0, 3 * ROWS_ONE)])
-    part = rows(half, HALF)
-    send(7, final.at[part], final.at[part], device(x, y, z, 1 - core))
+    slots = (slot_core, slot_one, slot_two, slot_last, staged)
+    finish = sum_blocks((x, y, z, core), device, packed, final, slots, sum_send, sum_recv)
 
     others = tiles.at[pl.ds(0, 63 * GR)]
     pltpu.make_async_copy(others, others, tile_recv).wait()
@@ -245,7 +306,7 @@
         energy = energy + tiles[i * GR:(i + 1) * GR, :]
     energy_ref[...] = energy
 
-    arrived(7, final.at[pl.ds(0, HALF)])
+    finish()
     result = pltpu.make_async_copy(final, gram_ref, own_sem)
     result.start()
 
@@ -256,14 +317,6 @@
     pltpu.make_async_copy(others, others, send_sem).wait()
     others = tiles.at[pl.ds(0, 63 * GR)]
     pltpu.make_async_copy(others, others, tile_send).wait()
-    left(0, slot_core)
-    left(1, slot_one.at[pl.ds(0, 3)])
-    left(2, slot_two.at[pl.ds(0, 3)])
-    left(3, slot_last.at[pl.ds(0, 7)])
-    left(4, final.at[pl.ds(0, 7 * ROWS_LAST)])
-    left(5, final.at[pl.ds(0, 3 * ROWS_TWO)])
-    left(6, final.at[pl.ds(0, 3 * ROWS_ONE)])
-    left(7, final.at[pl.ds(0, HALF)])
     result.wait()
 
 
@@ -277,31 +330,32 @@
             jax.ShapeDtypeStruct((GR, NB), jnp.float32),
             jax.ShapeDtypeStruct((N, WIDTH), jnp.bfloat16),
         ),
-        in_specs=[vmem, vmem, vmem, anywhere],
+        in_specs=[vmem, vmem, anywhere],
         out_specs=(anywhere, vmem, anywhere),
         scratch_shapes=[
             pltpu.VMEM((N, WIDTH), jnp.bfloat16),
             pltpu.VMEM((PACKED, NB), jnp.float32),
             pltpu.VMEM((PACKED, NB), jnp.float32),
             pltpu.VMEM((64 * GR, NB), jnp.float32),
-            pltpu.VMEM((HALF, NB), jnp.float32),
-            pltpu.VMEM((4, ROWS_ONE, NB), jnp.float32),
-            pltpu.VMEM((4, ROWS_TWO, NB), jnp.float32),
-            pltpu.VMEM((8, 2 * ROWS_LAST, NB), jnp.float32),
+            pltpu.VMEM((2, ROWS_CORE, NB), jnp.float32),
+            pltpu.VMEM((2, 4, ROWS_ONE, NB), jnp.float32),
+            pltpu.VMEM((2, 4, ROWS_TWO, NB), jnp.float32),
+            pltpu.VMEM((2, 8, 2 * ROWS_LAST, NB), jnp.float32),
+            pltpu.VMEM((2, 8, 2 * ROWS_LAST, NB), jnp.float32),
             pltpu.SemaphoreType.DMA,
             pltpu.SemaphoreType.DMA((PIECES,)),
             pltpu.SemaphoreType.DMA,
             pltpu.SemaphoreType.DMA,
             pltpu.SemaphoreType.DMA,
             pltpu.SemaphoreType.DMA((PIECES,)),
-            pltpu.SemaphoreType.DMA((8,)),
-            pltpu.SemaphoreType.DMA((8,)),
+            pltpu.SemaphoreType.DMA((2 * STEPS,)),
+            pltpu.SemaphoreType.DMA((2 * STEPS,)),
         ],
         compiler_params=pltpu.CompilerParams(
             collective_id=0, has_side_effects=True, vmem_limit_bytes=48 * 1024 * 1024
         ),
         name="gram",
-    )(spin_bits, bond_weights().astype(jnp.bfloat16), flip_energy.reshape(PER, 1), jacobian)
+    )(spin_bits, flip_energy.reshape(1, PER), jacobian)
 
 
 def split3(x):

time: 244 us -> 238 us (0.975)
  Pallas kernels: 242 us -> 236 us
    pallas_call x1, Pallas kernels: 197 us -> 192 us  [gram_call(): pl.pallas_call(gram_kernel, out_shape=(jax.ShapeDtypeStruct((PACKED, NB),...]
where the time goes in v3:
time: 238 us
  Pallas kernels  236 us (99%)
    pallas_call x1, Pallas kernels, gram_call(): pl.pallas_call(gram_kernel, out_shape=(jax.ShapeDtypeStruct((PACKED, NB),...  192 us
    pallas_call x1, Pallas kernels, solve_call(): pl.pallas_call(solve_kernel, out_shape=jax.ShapeDtypeStruct((1, WIDTH), j...  44.6 us

profile of v3, /device:TPU:1, one launch (start us, length us, event | category | flops | bytes accessed | tf_op | source)
XLA Modules:
  0.0 237.6 jit_solution(11797967691794172654)
XLA Ops:
  0.0 0.0 copy-start
  0.0 0.7 copy-done
  0.7 0.0 copy-start.1
  0.7 0.7 copy-done.1
  1.4 191.6 %gram.1 = (f32[4608,128]{1,0:T(8,128)S(1)}, f32[8,128]{1,0:T(8,128)S(1)}, bf16[1024,3072]{1,0:T(8,128)(2,1)}) custom-call(s32[16,100]{1,0:T(8,128)S(1)} %copy-done, f32[1,16]{1,0:T(1,128)S(1)} %bitcast.2, bf16[16,196608]{1,0:T(8,128)(2,1)} %jac_ref.1), custom_call_target="tpu_custom_call" | custom-call | tf_op jit(solution)/shard_map/gram/pallas_call | solution.py:326
  193.0 44.6 %solve.1 = f32[1,3072]{1,0:T(1,128)} custom-call(f32[4608,128]{1,0:T(8,128)S(1)} %get-tuple-element.8.gram_ref, f32[8,128]{1,0:T(8,128)S(1)} %get-tuple-element.9.energy_ref, bf16[1024,3072]{1,0:T(8,128)(2,1)} %get-tuple-element.10.centred_ref), custom_call_target="tpu_custom_call" | custom-call | tf_op jit(solution)/shard_map/solve/pallas_call | solution.py:482
Async XLA Ops:
  0.0 0.7 copy-start
  0.7 0.7 copy-start.1

commit v4 on v3

--- a/solution.py
+++ b/solution.py
@@ -383,34 +383,62 @@
     return jnp.broadcast_to(v[r:r + 1, :], (GR, NB))
 
 
+def add_all(terms):
+    while len(terms) > 1:
+        terms = [terms[i] + terms[i + 1] for i in range(0, len(terms), 2)]
+    return terms[0]
+
+
 def invert_block(rows):
     lane = lax.broadcasted_iota(jnp.int32, (GR, NB), 1)
     sub = lax.broadcasted_iota(jnp.int32, (GR, NB), 0)
     count = NB // GR
-    for g in range(count):
-        base = g * GR
-        own = rows[g]
-        piv_cols = [lanes(own, base + c) for c in range(GR)]
-        in_piv = (lane >= base) & (lane < base + GR)
-        row = jnp.where(in_piv, jnp.where(lane - base == sub, 1.0, 0.0), own)
-        for q in range(GR):
-            at = sub == q
-            inv = 1.0 / subs(piv_cols[q], q)
-            coef = jnp.where(at, -inv, piv_cols[q] * inv)
-            row = jnp.where(at, 0.0, row) - coef * subs(row, q)
-            for c in range(q + 1, GR):
-                piv_cols[c] = jnp.where(at, 0.0, piv_cols[c]) - coef * subs(piv_cols[c], q)
-        spread = [subs(row, q) for q in range(GR)]
-        new_rows = []
-        for v in range(count):
-            if v == g:
-                new_rows.append(row)
-                continue
-            terms = [lanes(rows[v], base + q) * spread[q] for q in range(GR)]
-            total = (((terms[0] + terms[1]) + (terms[2] + terms[3]))
-                     + ((terms[4] + terms[5]) + (terms[6] + terms[7])))
-            new_rows.append(jnp.where(in_piv, 0.0, rows[v]) - total)
-        rows = new_rows
+    width = count // 2
+    for low in range(0, count, width):
+        high = low + width
+        piv = [lanes(rows[low], low * GR + c) for c in range(GR)]
+        for g in range(low, high):
+            base = g * GR
+            own = rows[g]
+            more = g + 1 < high
+            ahead = []
+            if more:
+                ahead = [lanes(own, base + GR + c) for c in range(GR)]
+                coef_next = [lanes(rows[g + 1], base + q) for q in range(GR)]
+                piv_next = [lanes(rows[g + 1], base + GR + c) for c in range(GR)]
+            in_piv = (lane >= base) & (lane < base + GR)
+            row = jnp.where(in_piv, jnp.where(lane - base == sub, 1.0, 0.0), own)
+            for q in range(GR):
+                at = sub == q
+                inv = 1.0 / subs(piv[q], q)
+                signed = jnp.where(at, -1.0, piv[q])
+                coef = signed * inv
+                if q + 1 < GR:
+                    piv[q + 1] = jnp.where(at, 0.0, piv[q + 1]) - (signed * subs(piv[q + 1], q)) * inv
+                for c in range(q + 2, GR):
+                    piv[c] = jnp.where(at, 0.0, piv[c]) - coef * subs(piv[c], q)
+                row = jnp.where(at, 0.0, row) - coef * subs(row, q)
+                ahead = [jnp.where(at, 0.0, a) - coef * subs(a, q) for a in ahead]
+            spread = [subs(row, q) for q in range(GR)]
+            if more:
+                piv = [
+                    piv_next[c] - add_all([coef_next[q] * subs(ahead[c], q) for q in range(GR)]) for c in range(GR)
+                ]
+            new_rows = list(rows)
+            new_rows[g] = row
+            for v in range(low, high):
+                if v == g:
+                    continue
+                coefs = coef_next if more and v == g + 1 else [lanes(rows[v], base + q) for q in range(GR)]
+                new_rows[v] = jnp.where(in_piv, 0.0, rows[v]) - add_all([coefs[q] * spread[q] for q in range(GR)])
+            rows = new_rows
+        whole = jnp.concatenate(rows, axis=0)
+        rest = jnp.concatenate(rows[:low] + rows[high:], axis=0)
+        wide_lane = lax.broadcasted_iota(jnp.int32, rest.shape, 1)
+        inside = (wide_lane >= low * GR) & (wide_lane < high * GR)
+        rest = jnp.where(inside, 0.0, rest) - dot_wide(jnp.where(inside, rest, 0.0), whole)
+        parts = [rest[i * GR:(i + 1) * GR, :] for i in range(count - width)]
+        rows = parts[:low] + rows[low:high] + parts[low:]
     return rows
 
 

time: 238 us -> 231 us (0.971)
  Pallas kernels: 236 us -> 230 us
    pallas_call x1, Pallas kernels: 44.6 us -> 38.1 us  [solve_call(): pl.pallas_call(solve_kernel, out_shape=jax.ShapeDtypeStruct((1, WIDTH), j...]
where the time goes in v4:
time: 231 us
  Pallas kernels  230 us (100%)
    pallas_call x1, Pallas kernels, gram_call(): pl.pallas_call(gram_kernel, out_shape=(jax.ShapeDtypeStruct((PACKED, NB),...  192 us
    pallas_call x1, Pallas kernels, solve_call(): pl.pallas_call(solve_kernel, out_shape=jax.ShapeDtypeStruct((1, WIDTH), j...  38.1 us

profile of v4, /device:TPU:1, one launch (start us, length us, event | category | flops | bytes accessed | tf_op | source)
XLA Modules:
  0.0 231.1 jit_solution(3449574103439517479)
XLA Ops:
  0.0 0.0 copy-start
  0.0 0.7 copy-done
  0.7 0.0 copy-start.1
  0.7 0.7 copy-done.1
  1.4 191.6 %gram.1 = (f32[4608,128]{1,0:T(8,128)S(1)}, f32[8,128]{1,0:T(8,128)S(1)}, bf16[1024,3072]{1,0:T(8,128)(2,1)}) custom-call(s32[16,100]{1,0:T(8,128)S(1)} %copy-done, f32[1,16]{1,0:T(1,128)S(1)} %bitcast.2, bf16[16,196608]{1,0:T(8,128)(2,1)} %jac_ref.1), custom_call_target="tpu_custom_call" | custom-call | tf_op jit(solution)/shard_map/gram/pallas_call | solution.py:326
  193.0 38.1 %solve.1 = f32[1,3072]{1,0:T(1,128)} custom-call(f32[4608,128]{1,0:T(8,128)S(1)} %get-tuple-element.8.gram_ref, f32[8,128]{1,0:T(8,128)S(1)} %get-tuple-element.9.energy_ref, bf16[1024,3072]{1,0:T(8,128)(2,1)} %get-tuple-element.10.centred_ref), custom_call_target="tpu_custom_call" | custom-call | tf_op jit(solution)/shard_map/solve/pallas_call | solution.py:510
Async XLA Ops:
  0.0 0.7 copy-start
  0.7 0.7 copy-start.1

commit v5 on v3

--- a/solution.py
+++ b/solution.py
@@ -163,25 +163,185 @@
         own = final.at[rows(half, ROWS_CORE)]
         send(part, 7, own, own, other_core)
 
-    for move in (to_core, to_one, to_two, to_last, back_last, back_two, back_one, back_core):
-        for part in range(2):
-            move(part)
+    moves = (to_core, to_one, to_two, to_last, back_last, back_two, back_one, back_core)
+
+    def first_half():
+        for at in range(STEPS):
+            moves[at](0)
+            if at:
+                moves[at - 1](1)
+        arrived(0, STEPS - 1)
+
+    def second_half():
+        moves[STEPS - 1](1)
+        arrived(1, STEPS - 1)
 
     def finish():
         for part in range(2):
-            arrived(part, 7)
             for step in range(STEPS):
                 like = likes(part)[step]
                 pltpu.make_async_copy(like, like, sum_send.at[part * STEPS + step]).wait()
 
-    return finish
-
-
-def gram_kernel(
-    spin_ref, flip_ref, jac_ref,
-    gram_ref, energy_ref, centred_ref,
-    held, packed, final, tiles, slot_core, slot_one, slot_two, slot_last, staged,
-    send_sem, recv_sem, own_sem, tile_send, tile_recv, out_sem, sum_send, sum_recv,
+    return first_half, second_half, finish
+
+
+def split3(x):
+    high = x.astype(jnp.bfloat16)
+    rest = x - high.astype(jnp.float32)
+    mid = rest.astype(jnp.bfloat16)
+    low = (rest - mid.astype(jnp.float32)).astype(jnp.bfloat16)
+    return high, mid, low
+
+
+def dot_wide(a, b, turned=False):
+    ah, am, al = split3(a)
+    bh, bm, bl = split3(b)
+    left = jnp.concatenate([ah, ah, am, am, ah, al], axis=1)
+    right = jnp.concatenate([bh, bm, bh, bm, bl, bh], axis=1 if turned else 0)
+    dims = (((1,), (1 if turned else 0,)), ((), ()))
+    return lax.dot_general(left, right, dims, preferred_element_type=jnp.float32)
+
+
+def lanes(v, c):
+    return jnp.broadcast_to(v[:, c:c + 1], (GR, NB))
+
+
+def subs(v, r):
+    return jnp.broadcast_to(v[r:r + 1, :], (GR, NB))
+
+
+def add_all(terms):
+    while len(terms) > 1:
+        terms = [terms[i] + terms[i + 1] for i in range(0, len(terms), 2)]
+    return terms[0]
+
+
+def invert_block(rows):
+    lane = lax.broadcasted_iota(jnp.int32, (GR, NB), 1)
+    sub = lax.broadcasted_iota(jnp.int32, (GR, NB), 0)
+    count = NB // GR
+    width = count // 2
+    for low in range(0, count, width):
+        high = low + width
+        piv = [lanes(rows[low], low * GR + c) for c in range(GR)]
+        for g in range(low, high):
+            base = g * GR
+            own = rows[g]
+            more = g + 1 < high
+            ahead = []
+            if more:
+                ahead = [lanes(own, base + GR + c) for c in range(GR)]
+                coef_next = [lanes(rows[g + 1], base + q) for q in range(GR)]
+                piv_next = [lanes(rows[g + 1], base + GR + c) for c in range(GR)]
+            in_piv = (lane >= base) & (lane < base + GR)
+            row = jnp.where(in_piv, jnp.where(lane - base == sub, 1.0, 0.0), own)
+            for q in range(GR):
+                at = sub == q
+                inv = 1.0 / subs(piv[q], q)
+                signed = jnp.where(at, -1.0, piv[q])
+                coef = signed * inv
+                if q + 1 < GR:
+                    piv[q + 1] = jnp.where(at, 0.0, piv[q + 1]) - (signed * subs(piv[q + 1], q)) * inv
+                for c in range(q + 2, GR):
+                    piv[c] = jnp.where(at, 0.0, piv[c]) - coef * subs(piv[c], q)
+                row = jnp.where(at, 0.0, row) - coef * subs(row, q)
+                ahead = [jnp.where(at, 0.0, a) - coef * subs(a, q) for a in ahead]
+            spread = [subs(row, q) for q in range(GR)]
+            if more:
+                piv = [
+                    piv_next[c] - add_all([coef_next[q] * subs(ahead[c], q) for q in range(GR)]) for c in range(GR)
+                ]
+            new_rows = list(rows)
+            new_rows[g] = row
+            for v in range(low, high):
+                if v == g:
+                    continue
+                coefs = coef_next if more and v == g + 1 else [lanes(rows[v], base + q) for q in range(GR)]
+                new_rows[v] = jnp.where(in_piv, 0.0, rows[v]) - add_all([coefs[q] * spread[q] for q in range(GR)])
+            rows = new_rows
+        whole = jnp.concatenate(rows, axis=0)
+        rest = jnp.concatenate(rows[:low] + rows[high:], axis=0)
+        wide_lane = lax.broadcasted_iota(jnp.int32, rest.shape, 1)
+        inside = (wide_lane >= low * GR) & (wide_lane < high * GR)
+        rest = jnp.where(inside, 0.0, rest) - dot_wide(jnp.where(inside, rest, 0.0), whole)
+        parts = [rest[i * GR:(i + 1) * GR, :] for i in range(count - width)]
+        rows = parts[:low] + rows[low:high] + parts[low:]
+    return rows
+
+
+def solve(energy, second_half, final, held, work, x_row, x_col):
+    sub = lax.broadcasted_iota(jnp.int32, (NB, NB), 0)
+    lane = lax.broadcasted_iota(jnp.int32, (NB, NB), 1)
+    eye = jnp.where(sub == lane, 1.0, 0.0)
+
+    def unpack(part):
+        blocks = [(i, j) for j in range(BLOCKS) for i in range(j, BLOCKS)]
+        for i, j in blocks[part * len(blocks) // 2:(part + 1) * len(blocks) // 2]:
+            block = final[block_at(i, j), :]
+            work[i * NB:(i + 1) * NB, j * NB:(j + 1) * NB] = block + 0.5 * eye if i == j else block
+
+    unpack(0)
+    tile = energy
+    mean = jnp.sum(jnp.sum(tile, axis=1, keepdims=True), axis=0, keepdims=True) * (1.0 / N)
+    tile = tile - mean
+    for i in range(BLOCKS):
+        work[N:N + GR, i * NB:(i + 1) * NB] = subs(tile, i)
+
+    def stage(k, carry):
+        at = pl.ds(pl.multiple_of(k * NB, NB), NB)
+        rows = [work[pl.ds(pl.multiple_of(k * NB + v * GR, GR), GR), at] for v in range(NB // GR)]
+        rows = invert_block(rows)
+        for v in range(NB // GR):
+            work[pl.ds(pl.multiple_of(k * NB + v * GR, GR), GR), at] = rows[v]
+
+        @pl.when(k == 0)
+        def _():
+            second_half()
+            unpack(1)
+
+        for c in range(BLOCKS - 1):
+            @pl.when(k == c)
+            def _():
+                own = slice(c * NB, (c + 1) * NB)
+                after = slice((c + 1) * NB, N)
+                below = slice((c + 1) * NB, N + GR)
+                turned = dot_wide(work[own, own], work[after, own], turned=True)
+                work[below, after] = work[below, after] - dot_wide(work[below, own], turned)
+                work[own, after] = turned
+        return carry
+
+    lax.fori_loop(0, BLOCKS, stage, 0)
+
+    for k in range(BLOCKS - 1, -1, -1):
+        own = slice(k * NB, (k + 1) * NB)
+        total = work[own, own] * work[N:N + 1, own]
+        for j in range(k + 1, BLOCKS):
+            col = slice(j * NB, (j + 1) * NB)
+            total = total - work[own, col] * x_row[0:1, col]
+        column = jnp.sum(total, axis=1, keepdims=True)
+        column = jnp.broadcast_to(column, (NB, NB))
+        x_row[0:1, own] = jnp.sum(column * eye, axis=0, keepdims=True)
+        x_col[own, :] = column.astype(jnp.bfloat16).astype(jnp.float32)
+
+    wide = x_row[0:1, :].astype(jnp.bfloat16).astype(jnp.float32)
+
+    acc = jnp.zeros((NB, NB), jnp.float32)
+    for i in range(BLOCKS):
+        part = final[block_at(i, i), :] * (0.5 * wide[:, i * NB:(i + 1) * NB])
+        for j in range(i):
+            part = part + final[block_at(i, j), :] * wide[:, j * NB:(j + 1) * NB]
+        acc = acc + part * x_col[i * NB:(i + 1) * NB, :]
+    square_sum = 2.0 * jnp.sum(jnp.sum(acc, axis=0, keepdims=True), axis=1, keepdims=True)
+    root_mean = jnp.sqrt(jnp.maximum(square_sum, 0.0) / PARAMS + 1e-06)
+    left = jnp.where(lax.broadcasted_iota(jnp.int32, (PER, N), 0) == 0, wide, 0.0).astype(jnp.bfloat16)
+    direction = jnp.dot(left, held[...], preferred_element_type=jnp.float32)
+    return -direction[0:1, :] / root_mean
+
+
+def update_kernel(
+    spin_any, flip_any, jac_ref, out_ref,
+    spin_ref, flip_ref, held, packed, final, tiles, slot_core, slot_one, slot_two, slot_last, staged, work, x_row, x_col,
+    send_sem, recv_sem, own_sem, spin_sem, flip_sem, tile_send, tile_recv, sum_send, sum_recv,
 ):
     samp, par = lax.axis_index("samp"), lax.axis_index("par")
     core = par % 2
@@ -191,6 +351,10 @@
     def device(x_at, y_at, z_at, core_at):
         return {"samp": (x_at // 2) * 32 + y_at * 8 + z_at, "par": (x_at % 2) * 2 + core_at}
 
+    spins = pltpu.make_async_copy(spin_any, spin_ref, spin_sem)
+    spins.start()
+    flips = pltpu.make_async_copy(flip_any, flip_ref, flip_sem)
+    flips.start()
     barrier = pltpu.get_barrier_semaphore()
 
     def greet(step, carry):
@@ -208,6 +372,9 @@
         jac_ref.at[:, pl.ds(pl.multiple_of(samp * WIDTH, NB), WIDTH)], held.at[mine], own_sem
     )
     own.start()
+    packed[...] = jnp.zeros_like(packed)
+    spins.wait()
+    flips.wait()
 
     signs = (2 * spin_ref[...] - 1).astype(jnp.float32).astype(jnp.bfloat16)
     linked = jnp.dot(signs, bond_weights().astype(jnp.bfloat16), preferred_element_type=jnp.float32)
@@ -262,7 +429,6 @@
     lax.fori_loop(0, 8 * PIECES, send_plane, 0)
     lax.fori_loop(1, 64, send_tile, 0)
     own.wait()
-    packed[...] = jnp.zeros_like(packed)
 
     def work_piece(piece, carry):
         cols = pl.ds(pl.multiple_of(piece * PIECE, NB), PIECE)
@@ -281,7 +447,6 @@
             return carry
 
         lax.fori_loop(0, N // PER, centre_rows, 0, unroll=4)
-        pltpu.make_async_copy(held.at[:, cols], centred_ref.at[:, cols], out_sem.at[piece]).start()
         for i in range(0, BLOCKS, 2):
             size = (i + 2) * NB
             product = lax.dot_general(
@@ -297,42 +462,35 @@
     lax.fori_loop(0, PIECES, work_piece, 0)
 
     slots = (slot_core, slot_one, slot_two, slot_last, staged)
-    finish = sum_blocks((x, y, z, core), device, packed, final, slots, sum_send, sum_recv)
+    first_half, second_half, finish = sum_blocks((x, y, z, core), device, packed, final, slots, sum_send, sum_recv)
+    first_half()
 
     others = tiles.at[pl.ds(0, 63 * GR)]
     pltpu.make_async_copy(others, others, tile_recv).wait()
     energy = tiles[0:GR, :]
     for i in range(1, 64):
         energy = energy + tiles[i * GR:(i + 1) * GR, :]
-    energy_ref[...] = energy
-
-    finish()
-    result = pltpu.make_async_copy(final, gram_ref, own_sem)
-    result.start()
-
-    for piece in range(PIECES):
-        cols = pl.ds(piece * PIECE, PIECE)
-        pltpu.make_async_copy(held.at[:, cols], centred_ref.at[:, cols], out_sem.at[piece]).wait()
+
+    direction = solve(energy, second_half, final, held, work, x_row, x_col)
+    out_ref[...] = direction
+
     others = held.at[pl.ds(0, N - PER)]
     pltpu.make_async_copy(others, others, send_sem).wait()
     others = tiles.at[pl.ds(0, 63 * GR)]
     pltpu.make_async_copy(others, others, tile_send).wait()
-    result.wait()
-
-
-def gram_call(spin_bits, flip_energy, jacobian):
-    vmem = pl.BlockSpec(memory_space=pltpu.VMEM)
+    finish()
+
+
+def update_call(spin_bits, flip_energy, jacobian):
     anywhere = pl.BlockSpec(memory_space=pl.ANY)
     return pl.pallas_call(
-        gram_kernel,
-        out_shape=(
-            jax.ShapeDtypeStruct((PACKED, NB), jnp.float32),
-            jax.ShapeDtypeStruct((GR, NB), jnp.float32),
-            jax.ShapeDtypeStruct((N, WIDTH), jnp.bfloat16),
-        ),
-        in_specs=[vmem, vmem, anywhere],
-        out_specs=(anywhere, vmem, anywhere),
+        update_kernel,
+        out_shape=jax.ShapeDtypeStruct((1, WIDTH), jnp.float32),
+        in_specs=[anywhere, anywhere, anywhere],
+        out_specs=pl.BlockSpec(memory_space=pltpu.VMEM),
         scratch_shapes=[
+            pltpu.VMEM((PER, SITES), jnp.int32),
+            pltpu.VMEM((1, PER), jnp.float32),
             pltpu.VMEM((N, WIDTH), jnp.bfloat16),
             pltpu.VMEM((PACKED, NB), jnp.float32),
             pltpu.VMEM((PACKED, NB), jnp.float32),
@@ -342,163 +500,28 @@
             pltpu.VMEM((2, 4, ROWS_TWO, NB), jnp.float32),
             pltpu.VMEM((2, 8, 2 * ROWS_LAST, NB), jnp.float32),
             pltpu.VMEM((2, 8, 2 * ROWS_LAST, NB), jnp.float32),
+            pltpu.VMEM((N + GR, N), jnp.float32),
+            pltpu.VMEM((GR, N), jnp.float32),
+            pltpu.VMEM((N, NB), jnp.float32),
             pltpu.SemaphoreType.DMA,
             pltpu.SemaphoreType.DMA((PIECES,)),
             pltpu.SemaphoreType.DMA,
             pltpu.SemaphoreType.DMA,
             pltpu.SemaphoreType.DMA,
-            pltpu.SemaphoreType.DMA((PIECES,)),
+            pltpu.SemaphoreType.DMA,
+            pltpu.SemaphoreType.DMA,
             pltpu.SemaphoreType.DMA((2 * STEPS,)),
             pltpu.SemaphoreType.DMA((2 * STEPS,)),
         ],
         compiler_params=pltpu.CompilerParams(
-            collective_id=0, has_side_effects=True, vmem_limit_bytes=48 * 1024 * 1024
+            collective_id=0, has_side_effects=True, vmem_limit_bytes=60 * 1024 * 1024
         ),
-        name="gram",
+        name="update",
     )(spin_bits, flip_energy.reshape(1, PER), jacobian)
 
 
-def split3(x):
-    high = x.astype(jnp.bfloat16)
-    rest = x - high.astype(jnp.float32)
-    mid = rest.astype(jnp.bfloat16)
-    low = (rest - mid.astype(jnp.float32)).astype(jnp.bfloat16)
-    return high, mid, low
-
-
-def dot_wide(a, b, turned=False):
-    ah, am, al = split3(a)
-    bh, bm, bl = split3(b)
-    left = jnp.concatenate([ah, ah, am, am, ah, al], axis=1)
-    right = jnp.concatenate([bh, bm, bh, bm, bl, bh], axis=1 if turned else 0)
-    dims = (((1,), (1 if turned else 0,)), ((), ()))
-    return lax.dot_general(left, right, dims, preferred_element_type=jnp.float32)
-
-
-def lanes(v, c):
-    return jnp.broadcast_to(v[:, c:c + 1], (GR, NB))
-
-
-def subs(v, r):
-    return jnp.broadcast_to(v[r:r + 1, :], (GR, NB))
-
-
-def invert_block(rows):
-    lane = lax.broadcasted_iota(jnp.int32, (GR, NB), 1)
-    sub = lax.broadcasted_iota(jnp.int32, (GR, NB), 0)
-    count = NB // GR
-    for g in range(count):
-        base = g * GR
-        own = rows[g]
-        piv_cols = [lanes(own, base + c) for c in range(GR)]
-        in_piv = (lane >= base) & (lane < base + GR)
-        row = jnp.where(in_piv, jnp.where(lane - base == sub, 1.0, 0.0), own)
-        for q in range(GR):
-            at = sub == q
-            inv = 1.0 / subs(piv_cols[q], q)
-            coef = jnp.where(at, -inv, piv_cols[q] * inv)
-            row = jnp.where(at, 0.0, row) - coef * subs(row, q)
-            for c in range(q + 1, GR):
-                piv_cols[c] = jnp.where(at, 0.0, piv_cols[c]) - coef * subs(piv_cols[c], q)
-        spread = [subs(row, q) for q in range(GR)]
-        new_rows = []
-        for v in range(count):
-            if v == g:
-                new_rows.append(row)
-                continue
-            terms = [lanes(rows[v], base + q) * spread[q] for q in range(GR)]
-            total = (((terms[0] + terms[1]) + (terms[2] + terms[3]))
-                     + ((terms[4] + terms[5]) + (terms[6] + terms[7])))
-            new_rows.append(jnp.where(in_piv, 0.0, rows[v]) - total)
-        rows = new_rows
-    return rows
-
-
-def solve_kernel(gram_ref, energy_ref, centred_ref, out_ref, work, held, x_row, x_col, sem):
-    fetch = pltpu.make_async_copy(centred_ref, held, sem)
-    fetch.start()
-    sub = lax.broadcasted_iota(jnp.int32, (NB, NB), 0)
-    lane = lax.broadcasted_iota(jnp.int32, (NB, NB), 1)
-    eye = jnp.where(sub == lane, 1.0, 0.0)
-    for i in range(BLOCKS):
-        at = slice(i * NB, (i + 1) * NB)
-        for j in range(i):
-            work[at, j * NB:(j + 1) * NB] = gram_ref[block_at(i, j), :]
-        work[at, at] = gram_ref[block_at(i, i), :] + 0.5 * eye
-    tile = energy_ref[...]
-    mean = jnp.sum(jnp.sum(tile, axis=1, keepdims=True), axis=0, keepdims=True) * (1.0 / N)
-    tile = tile - mean
-    for i in range(BLOCKS):
-        work[N:N + GR, i * NB:(i + 1) * NB] = subs(tile, i)
-
-    def stage(k, carry):
-        at = pl.ds(pl.multiple_of(k * NB, NB), NB)
-        rows = [work[pl.ds(pl.multiple_of(k * NB + v * GR, GR), GR), at] for v in range(NB // GR)]
-        rows = invert_block(rows)
-        for v in range(NB // GR):
-            work[pl.ds(pl.multiple_of(k * NB + v * GR, GR), GR), at] = rows[v]
-        for c in range(BLOCKS - 1):
-            @pl.when(k == c)
-            def _():
-                own = slice(c * NB, (c + 1) * NB)
-                after = slice((c + 1) * NB, N)
-                below = slice((c + 1) * NB, N + GR)
-                turned = dot_wide(work[own, own], work[after, own], turned=True)
-                work[below, after] = work[below, after] - dot_wide(work[below, own], turned)
-                work[own, after] = turned
-        return carry
-
-    lax.fori_loop(0, BLOCKS, stage, 0)
-
-    for k in range(BLOCKS - 1, -1, -1):
-        own = slice(k * NB, (k + 1) * NB)
-        total = work[own, own] * work[N:N + 1, own]
-        for j in range(k + 1, BLOCKS):
-            col = slice(j * NB, (j + 1) * NB)
-            total = total - work[own, col] * x_row[0:1, col]
-        column = jnp.sum(total, axis=1, keepdims=True)
-        column = jnp.broadcast_to(column, (NB, NB))
-        x_row[0:1, own] = jnp.sum(column * eye, axis=0, keepdims=True)
-        x_col[own, :] = column.astype(jnp.bfloat16).astype(jnp.float32)
-
-    wide = x_row[0:1, :].astype(jnp.bfloat16).astype(jnp.float32)
-
-    acc = jnp.zeros((NB, NB), jnp.float32)
-    for i in range(BLOCKS):
-        part = gram_ref[block_at(i, i), :] * (0.5 * wide[:, i * NB:(i + 1) * NB])
-        for j in range(i):
-            part = part + gram_ref[block_at(i, j), :] * wide[:, j * NB:(j + 1) * NB]
-        acc = acc + part * x_col[i * NB:(i + 1) * NB, :]
-    square_sum = 2.0 * jnp.sum(jnp.sum(acc, axis=0, keepdims=True), axis=1, keepdims=True)
-    root_mean = jnp.sqrt(jnp.maximum(square_sum, 0.0) / PARAMS + 1e-06)
-    fetch.wait()
-    left = jnp.where(lax.broadcasted_iota(jnp.int32, (PER, N), 0) == 0, wide, 0.0).astype(jnp.bfloat16)
-    direction = jnp.dot(left, held[...], preferred_element_type=jnp.float32)
-    out_ref[...] = -direction[0:1, :] / root_mean
-
-
-def solve_call(gram, energy, centred):
-    vmem = pl.BlockSpec(memory_space=pltpu.VMEM)
-    return pl.pallas_call(
-        solve_kernel,
-        out_shape=jax.ShapeDtypeStruct((1, WIDTH), jnp.float32),
-        in_specs=[vmem, vmem, pl.BlockSpec(memory_space=pl.ANY)],
-        out_specs=vmem,
-        scratch_shapes=[
-            pltpu.VMEM((N + GR, N), jnp.float32),
-            pltpu.VMEM((N, WIDTH), jnp.bfloat16),
-            pltpu.VMEM((GR, N), jnp.float32),
-            pltpu.VMEM((N, NB), jnp.float32),
-            pltpu.SemaphoreType.DMA,
-        ],
-        compiler_params=pltpu.CompilerParams(vmem_limit_bytes=48 * 1024 * 1024),
-        name="solve",
-    )(gram, energy, centred)
-
-
 def on_device(spin_bits, flip_energy, jacobian):
-    gram, energy, centred = gram_call(spin_bits, flip_energy, jacobian)
-    return solve_call(gram, energy, centred).reshape(1, 1, -1)
+    return update_call(spin_bits, flip_energy, jacobian).reshape(1, 1, -1)
 
 
 def solution(mesh):

time: 238 us -> 230 us (0.966)
  Pallas kernels: 236 us -> 229 us
    pallas_call x2 -> x1, Pallas kernels: 236 us -> 229 us  [update_call(): pl.pallas_call(update_kernel, out_shape=jax.ShapeDtypeStruct((1, WIDTH),...]
where the time goes in v5:
time: 230 us
  Pallas kernels  229 us (100%)
    pallas_call x1, Pallas kernels, update_call(): pl.pallas_call(update_kernel, out_shape=jax.ShapeDtypeStruct((1, WIDTH),...  229 us

profile of v5, /device:TPU:1, one launch (start us, length us, event | category | flops | bytes accessed | tf_op | source)
XLA Modules:
  0.0 230.1 jit_solution(11556521325907421995)
XLA Ops:
  0.0 228.8 %update.1 = f32[1,3072]{1,0:T(1,128)} custom-call(s32[16,100]{1,0:T(8,128)} %spin_any.1, f32[1,16]{1,0:T(1,128)} %bitcast.3, bf16[16,196608]{1,0:T(8,128)(2,1)} %jac_ref.1), custom_call_target="tpu_custom_call" | custom-call | tf_op jit(solution)/shard_map/update/pallas_call | solution.py:486
  228.8 1.3 copy.5

commit v6 on v5

--- a/solution.py
+++ b/solution.py
@@ -166,14 +166,12 @@
     moves = (to_core, to_one, to_two, to_last, back_last, back_two, back_one, back_core)
 
     def first_half():
-        for at in range(STEPS):
-            moves[at](0)
-            if at:
-                moves[at - 1](1)
+        for move in moves:
+            for part in range(2):
+                move(part)
         arrived(0, STEPS - 1)
 
     def second_half():
-        moves[STEPS - 1](1)
         arrived(1, STEPS - 1)
 
     def finish():
@@ -253,9 +251,7 @@
                 ]
             new_rows = list(rows)
             new_rows[g] = row
-            for v in range(low, high):
-                if v == g:
-                    continue
+            for v in [*range(g + 1, high), *range(low, g)]:
                 coefs = coef_next if more and v == g + 1 else [lanes(rows[v], base + q) for q in range(GR)]
                 new_rows[v] = jnp.where(in_piv, 0.0, rows[v]) - add_all([coefs[q] * spread[q] for q in range(GR)])
             rows = new_rows
@@ -312,6 +308,7 @@
 
     lax.fori_loop(0, BLOCKS, stage, 0)
 
+    direction = jnp.zeros((PER, WIDTH), jnp.float32)
     for k in range(BLOCKS - 1, -1, -1):
         own = slice(k * NB, (k + 1) * NB)
         total = work[own, own] * work[N:N + 1, own]
@@ -322,6 +319,10 @@
         column = jnp.broadcast_to(column, (NB, NB))
         x_row[0:1, own] = jnp.sum(column * eye, axis=0, keepdims=True)
         x_col[own, :] = column.astype(jnp.bfloat16).astype(jnp.float32)
+        if k % 2 == 0:
+            pair = slice(k * NB, (k + 2) * NB)
+            weights = jnp.broadcast_to(x_row[0:1, pair], (PER, 2 * NB)).astype(jnp.bfloat16)
+            direction = direction + jnp.dot(weights, held[pair, :], preferred_element_type=jnp.float32)
 
     wide = x_row[0:1, :].astype(jnp.bfloat16).astype(jnp.float32)
 
@@ -333,8 +334,6 @@
         acc = acc + part * x_col[i * NB:(i + 1) * NB, :]
     square_sum = 2.0 * jnp.sum(jnp.sum(acc, axis=0, keepdims=True), axis=1, keepdims=True)
     root_mean = jnp.sqrt(jnp.maximum(square_sum, 0.0) / PARAMS + 1e-06)
-    left = jnp.where(lax.broadcasted_iota(jnp.int32, (PER, N), 0) == 0, wide, 0.0).astype(jnp.bfloat16)
-    direction = jnp.dot(left, held[...], preferred_element_type=jnp.float32)
     return -direction[0:1, :] / root_mean
 
 

time: 230 us -> 226 us (0.983)
  Pallas kernels: 229 us -> 224 us
    pallas_call x1, Pallas kernels: 229 us -> 224 us  [update_call(): pl.pallas_call(update_kernel, out_shape=jax.ShapeDtypeStruct((1, WIDTH),...]
where the time goes in v6:
time: 226 us; the launch traced here: 225 us
  Pallas kernels  224 us (99%)
    pallas_call x1, Pallas kernels, update_call(): pl.pallas_call(update_kernel, out_shape=jax.ShapeDtypeStruct((1, WIDTH),...  224 us

profile of v6, /device:TPU:1, one launch (start us, length us, event | category | flops | bytes accessed | tf_op | source)
XLA Modules:
  0.0 225.1 jit_solution(9612510601730533942)
XLA Ops:
  0.0 223.8 %update.1 = f32[1,3072]{1,0:T(1,128)} custom-call(s32[16,100]{1,0:T(8,128)} %spin_any.1, f32[1,16]{1,0:T(1,128)} %bitcast.3, bf16[16,196608]{1,0:T(8,128)(2,1)} %jac_ref.1), custom_call_target="tpu_custom_call" | custom-call | tf_op jit(solution)/shard_map/update/pallas_call | solution.py:485
  223.8 1.3 copy.5

commit v7 on v6

--- a/solution.py
+++ b/solution.py
@@ -15,7 +15,7 @@
 PARAMS = 786432
 PER = 16
 WIDTH = 3072
-PIECES = 4
+PIECES = 6
 PIECE = WIDTH // PIECES
 PACKED = BLOCKS * (BLOCKS + 1) // 2 * NB
 HALF = PACKED // 2
@@ -165,11 +165,14 @@
 
     moves = (to_core, to_one, to_two, to_last, back_last, back_two, back_one, back_core)
 
-    def first_half():
+    def first_half(between):
         for move in moves:
             for part in range(2):
                 move(part)
+            if move is to_last:
+                result = between()
         arrived(0, STEPS - 1)
+        return result
 
     def second_half():
         arrived(1, STEPS - 1)
@@ -462,21 +465,22 @@
 
     slots = (slot_core, slot_one, slot_two, slot_last, staged)
     first_half, second_half, finish = sum_blocks((x, y, z, core), device, packed, final, slots, sum_send, sum_recv)
-    first_half()
-
-    others = tiles.at[pl.ds(0, 63 * GR)]
-    pltpu.make_async_copy(others, others, tile_recv).wait()
-    energy = tiles[0:GR, :]
-    for i in range(1, 64):
-        energy = energy + tiles[i * GR:(i + 1) * GR, :]
-
+
+    def between():
+        others = held.at[pl.ds(0, N - PER)]
+        pltpu.make_async_copy(others, others, send_sem).wait()
+        others = tiles.at[pl.ds(0, 63 * GR)]
+        pltpu.make_async_copy(others, others, tile_send).wait()
+        pltpu.make_async_copy(others, others, tile_recv).wait()
+        energy = tiles[0:GR, :]
+        for i in range(1, 64):
+            energy = energy + tiles[i * GR:(i + 1) * GR, :]
+        return energy
+
+    energy = first_half(between)
     direction = solve(energy, second_half, final, held, work, x_row, x_col)
     out_ref[...] = direction
 
-    others = held.at[pl.ds(0, N - PER)]
-    pltpu.make_async_copy(others, others, send_sem).wait()
-    others = tiles.at[pl.ds(0, 63 * GR)]
-    pltpu.make_async_copy(others, others, tile_send).wait()
     finish()
 
 

time: 226 us -> 224 us (level)
  no operation moved by 1% of the time
where the time goes in v7:
time: 224 us; the launch traced here: 223 us
  Pallas kernels  222 us (99%)
    pallas_call x1, Pallas kernels, update_call(): pl.pallas_call(update_kernel, out_shape=jax.ShapeDtypeStruct((1, WIDTH),...  222 us

profile of v7, /device:TPU:1, one launch (start us, length us, event | category | flops | bytes accessed | tf_op | source)
XLA Modules:
  0.0 223.4 jit_solution(13058232979144852957)
XLA Ops:
  0.0 222.1 %update.1 = f32[1,3072]{1,0:T(1,128)} custom-call(s32[16,100]{1,0:T(8,128)} %spin_any.1, f32[1,16]{1,0:T(1,128)} %bitcast.3, bf16[16,196608]{1,0:T(8,128)(2,1)} %jac_ref.1), custom_call_target="tpu_custom_call" | custom-call | tf_op jit(solution)/shard_map/update/pallas_call | solution.py:489
  222.1 1.3 copy.5

commit v8 on v7

--- a/solution.py
+++ b/solution.py
@@ -87,6 +87,10 @@
         like = likes(part)[step]
         pltpu.make_async_copy(like, like, sum_recv.at[part * STEPS + step]).wait()
 
+    def left(part, step):
+        like = likes(part)[step]
+        pltpu.make_async_copy(like, like, sum_send.at[part * STEPS + step]).wait()
+
     def starts(part):
         half = part * HALF + core * ROWS_CORE
         one = half + pos_one * ROWS_ONE
@@ -171,6 +175,9 @@
                 move(part)
             if move is to_last:
                 result = between()
+        for part in range(2):
+            for step in range(STEPS - 1):
+                left(part, step)
         arrived(0, STEPS - 1)
         return result
 
@@ -179,9 +186,7 @@
 
     def finish():
         for part in range(2):
-            for step in range(STEPS):
-                like = likes(part)[step]
-                pltpu.make_async_copy(like, like, sum_send.at[part * STEPS + step]).wait()
+            left(part, STEPS - 1)
 
     return first_half, second_half, finish
 
@@ -361,7 +366,7 @@
 
     def greet(step, carry):
         pl.semaphore_signal(
-            barrier, inc=1, device_id={"samp": lax.rem(samp + step, 64), "par": par}, device_id_type=MESH
+            barrier, inc=1, device_id={"samp": lax.rem(samp + 1 + lax.rem(step + 30, 63), 64), "par": par}, device_id_type=MESH
         )
         return carry
 

time: 224 us -> 224 us (level)
  no operation moved by 1% of the time
where the time goes in v8:
time: 224 us
  Pallas kernels  223 us (100%)
    pallas_call x1, Pallas kernels, update_call(): pl.pallas_call(update_kernel, out_shape=jax.ShapeDtypeStruct((1, WIDTH),...  223 us

profile of v8, /device:TPU:1, one launch (start us, length us, event | category | flops | bytes accessed | tf_op | source)
XLA Modules:
  0.0 224.1 jit_solution(5775763659568257485)
XLA Ops:
  0.0 222.8 %update.1 = f32[1,3072]{1,0:T(1,128)} custom-call(s32[16,100]{1,0:T(8,128)} %spin_any.1, f32[1,16]{1,0:T(1,128)} %bitcast.3, bf16[16,196608]{1,0:T(8,128)(2,1)} %jac_ref.1), custom_call_target="tpu_custom_call" | custom-call | tf_op jit(solution)/shard_map/update/pallas_call | solution.py:494
  222.8 1.3 copy.5
